TPU v7x, 32 devices: a whole 2x2x4 slice. The times are simulated.
32 devices in a mesh: dp: 2 (over x), chan: 16 (over z, y, core).
Axes of the slice: x: 2, y: 2, z: 4, core: 2. Of those that a mesh axis runs over, the one named last changes fastest.
Arguments:
- features: bfloat16 [2, 2048, 16, 128], P('dp', 'chan'), may hold values from -7 to 7
- w_one: bfloat16 [2048, 256], P('chan'), may hold values from -0.1875 to 0.1875
- w_atrous: bfloat16 [3, 9, 2048, 256], P(None, None, 'chan'), may hold values from -0.0625 to 0.0625
- w_pool: bfloat16 [2048, 256], P('chan'), may hold values from -0.1875 to 0.1875
- w_proj: bfloat16 [5, 256, 256], P(None, 'chan'), may hold values from -0.25 to 0.25
- gains: float32 [5, 256], P(None, 'chan'), may hold values from 0.1 to 1.9
- biases: float32 [5, 256], P(None, 'chan'), may hold values from -3 to 3
- out_grad: bfloat16 [2, 256, 16, 128], P('dp', 'chan'), may hold values from -6 to 6
Outputs:
- output: float32 [2, 256, 16, 128], P('dp', 'chan')
- features_grad: float32 [2, 2048, 16, 128], P('dp', 'chan')
- w_one_grad: float32 [2048, 256], P('chan')
- w_atrous_grad: float32 [3, 9, 2048, 256], P(None, None, 'chan')
- w_pool_grad: float32 [2048, 256], P('chan')
- w_proj_grad: float32 [5, 256, 256], P(None, 'chan')
- gains_grad: float32 [5, 256], P(None, 'chan')
- biases_grad: float32 [5, 256], P(None, 'chan')
All inputs are finite; a program needn't handle non-finite values.
Results may differ from a plain program's by a relative error of at most 0.009.
Values may be sent and summed in bfloat16 or wider, within the bound.
A program may use at most 128 MiB of HBM per device.

v0:
```python
import jax
import jax.numpy as jnp
from jax import lax
from jax.sharding import PartitionSpec as P

atrous_rates = (6, 12, 18)
norm_eps = 1e-05


def shifted(values, vertical, horizontal):
    margin = max(abs(vertical), abs(horizontal))
    if margin == 0:
        return values
    height = values.shape[-2]
    breadth = values.shape[-1]
    spacing = [(0, 0)] * (values.ndim - 2) + [(margin, margin), (margin, margin)]
    padded = jnp.pad(values, spacing)
    return padded[
        ...,
        margin + vertical : margin + vertical + height,
        margin + horizontal : margin + horizontal + breadth,
    ]


def tap_offsets(dilation):
    return [
        ((along_rows - 1) * dilation, (along_cols - 1) * dilation)
        for along_rows in range(3)
        for along_cols in range(3)
    ]


def make_patches(features, dilation):
    return jnp.stack(
        [shifted(features, vertical, horizontal) for vertical, horizontal in tap_offsets(dilation)]
    )


def silu_slope(values):
    sigmoid = jax.nn.sigmoid(values)
    return sigmoid * (1.0 + values * (1.0 - sigmoid))


def expand_tail(values, extra):
    return values.reshape(values.shape + (1,) * extra)


def local(features, w_one, w_atrous, w_pool, w_proj, gains, biases, out_grad):
    highest = lax.Precision.HIGHEST
    images, local_in, height, columns = features.shape
    pixels = height * columns
    population = images * pixels * lax.axis_size("dp")
    patches = jnp.stack([make_patches(features, dilation) for dilation in atrous_rates])
    pooled = jnp.sum(features, axis=(2, 3), dtype=jnp.float32) / pixels
    one_term = jnp.einsum("nchw,co->onhw", features, w_one, preferred_element_type=jnp.float32)
    rate_terms = jnp.einsum(
        "rtnchw,rtco->ronhw", patches, w_atrous, preferred_element_type=jnp.float32
    )
    spatial_term = jnp.concatenate([one_term[None], rate_terms])
    pool_term = jnp.dot(pooled, w_pool.astype(jnp.float32), precision=highest).T[None]
    branch_pre, pool_pre = (
        lax.psum_scatter(spatial_term, "chan", scatter_dimension=1, tiled=True),
        lax.psum_scatter(pool_term, "chan", scatter_dimension=1, tiled=True),
    )
    branch_totals, branch_squares = lax.psum(
        (jnp.sum(branch_pre, axis=(2, 3, 4)), jnp.sum(branch_pre * branch_pre, axis=(2, 3, 4))),
        "dp",
    )
    branch_mean = branch_totals / population
    branch_inv = lax.rsqrt(branch_squares / population - branch_mean * branch_mean + norm_eps)
    centred = branch_pre - expand_tail(branch_mean, 3)
    branch_z = centred * expand_tail(gains[:4] * branch_inv, 3) + expand_tail(biases[:4], 3)
    branch_hat = centred * expand_tail(branch_inv, 3)
    act_low = jax.nn.silu(branch_z).astype(jnp.bfloat16)
    pool_act = jax.nn.silu(pool_pre).astype(jnp.bfloat16)
    window = w_proj
    spatial = jnp.einsum("bonhw,bod->dnhw", act_low, window[:4], preferred_element_type=jnp.float32)
    pool_part = jnp.einsum("bon,bod->dn", pool_act, window[4:], preferred_element_type=jnp.float32)
    proj_pre = lax.psum_scatter(
        spatial + pool_part[:, :, None, None], "chan", scatter_dimension=0, tiled=True
    )
    proj_totals, proj_squares = lax.psum(
        (jnp.sum(proj_pre, axis=(1, 2, 3)), jnp.sum(proj_pre * proj_pre, axis=(1, 2, 3))), "dp"
    )
    proj_mean = proj_totals / population
    proj_inv = lax.rsqrt(proj_squares / population - proj_mean * proj_mean + norm_eps)
    proj_centred = proj_pre - expand_tail(proj_mean, 3)
    proj_z = proj_centred * expand_tail(gains[4] * proj_inv, 3) + expand_tail(biases[4], 3)
    proj_hat = proj_centred * expand_tail(proj_inv, 3)
    output = jnp.transpose(jax.nn.silu(proj_z), (1, 0, 2, 3))
    grad_out = jnp.transpose(out_grad, (1, 0, 2, 3)).astype(jnp.float32)
    proj_dz = grad_out * silu_slope(proj_z)
    proj_dbias, proj_dgain = lax.psum(
        (jnp.sum(proj_dz, axis=(1, 2, 3)), jnp.sum(proj_dz * proj_hat, axis=(1, 2, 3))), "dp"
    )
    proj_dpre = expand_tail(gains[4] * proj_inv, 3) * (
        proj_dz
        - expand_tail(proj_dbias / population, 3)
        - proj_hat * expand_tail(proj_dgain / population, 3)
    )
    proj_low = proj_dpre.astype(jnp.bfloat16)
    pool_act_wide = pool_act.astype(jnp.float32)
    portion = lax.all_gather(proj_low, "chan", axis=0, tiled=True)
    window = w_proj
    act_grad = jnp.einsum(
        "bod,dnhw->bonhw", window[:4], portion, preferred_element_type=jnp.float32
    )
    portion_sum = jnp.sum(portion, axis=(2, 3), dtype=jnp.float32)
    pool_grad = jnp.einsum(
        "bod,dn->bon", window[4:].astype(jnp.float32), portion_sum, precision=highest
    )
    spatial_part = jnp.einsum(
        "bonhw,dnhw->bod", act_low, portion, preferred_element_type=jnp.float32
    )
    pool_part = jnp.einsum("bon,dn->bod", pool_act_wide, portion_sum, precision=highest)
    weight_grad = jnp.concatenate([spatial_part, pool_part])
    act_grad, pool_grad, proj_wgrad = (act_grad, pool_grad, weight_grad)
    branch_dz = act_grad * silu_slope(branch_z)
    branch_dbias, branch_dgain = lax.psum(
        (jnp.sum(branch_dz, axis=(2, 3, 4)), jnp.sum(branch_dz * branch_hat, axis=(2, 3, 4))), "dp"
    )
    branch_dpre = expand_tail(gains[:4] * branch_inv, 3) * (
        branch_dz
        - expand_tail(branch_dbias / population, 3)
        - branch_hat * expand_tail(branch_dgain / population, 3)
    )
    branch_low = branch_dpre.astype(jnp.bfloat16)
    pool_low = (pool_grad * silu_slope(pool_pre)).astype(jnp.bfloat16)
    spatial_portion = lax.all_gather(branch_low, "chan", axis=1, tiled=True)
    pool_portion = lax.all_gather(pool_low, "chan", axis=1, tiled=True)
    pool_cols = w_pool.astype(jnp.float32)
    feature_grad = jnp.einsum(
        "co,onhw->nchw", w_one, spatial_portion[0], preferred_element_type=jnp.float32
    )
    patch_grad = jnp.einsum(
        "rtco,ronhw->rtnchw", w_atrous, spatial_portion[1:], preferred_element_type=jnp.float32
    )
    pool_wide = pool_portion[0].astype(jnp.float32)
    pooled_grad = jnp.dot(pool_wide.T, pool_cols.T, precision=highest)
    one_piece = jnp.einsum(
        "nchw,onhw->co", features, spatial_portion[0], preferred_element_type=jnp.float32
    )
    rate_piece = jnp.einsum(
        "rtnchw,ronhw->rtco", patches, spatial_portion[1:], preferred_element_type=jnp.float32
    )
    pool_piece = jnp.dot(pooled.T, pool_wide.T, precision=highest)
    one_grad = one_piece
    rate_grad = rate_piece
    pool_wgrad = pool_piece
    feature_grad, patch_grad, pooled_grad, one_grad, rate_grad, pool_wgrad = (
        feature_grad,
        patch_grad,
        pooled_grad,
        one_grad,
        rate_grad,
        pool_wgrad,
    )
    for branch, dilation in enumerate(atrous_rates):
        for tap_index, (vertical, horizontal) in enumerate(tap_offsets(dilation)):
            feature_grad = feature_grad + shifted(
                patch_grad[branch, tap_index], -vertical, -horizontal
            )
    feature_grad = feature_grad + (pooled_grad / pixels)[:, :, None, None]
    one_grad, rate_grad, pool_wgrad, proj_wgrad = (
        lax.psum(one_grad.astype(jnp.bfloat16), "dp").astype(jnp.float32),
        lax.psum(rate_grad.astype(jnp.bfloat16), "dp").astype(jnp.float32),
        lax.psum(pool_wgrad.astype(jnp.bfloat16), "dp").astype(jnp.float32),
        lax.psum(proj_wgrad.astype(jnp.bfloat16), "dp").astype(jnp.float32),
    )
    gains_grad = jnp.concatenate([branch_dgain, proj_dgain[None]])
    biases_grad = jnp.concatenate([branch_dbias, proj_dbias[None]])
    return (
        output,
        feature_grad,
        one_grad,
        rate_grad,
        pool_wgrad,
        proj_wgrad,
        gains_grad,
        biases_grad,
    )


def solution(mesh):
    placed = (
        P("dp", "chan", None, None),
        P("chan", None),
        P(None, None, "chan", None),
        P("chan", None),
        P(None, "chan", None),
        P(None, "chan"),
        P(None, "chan"),
        P("dp", "chan", None, None),
    )
    return jax.shard_map(
        local,
        mesh=mesh,
        in_specs=placed,
        out_specs=(
            P("dp", "chan", None, None),
            P("dp", "chan", None, None),
            P("chan", None),
            P(None, None, "chan", None),
            P("chan", None),
            P(None, "chan", None),
            P(None, "chan"),
            P(None, "chan"),
        ),
        check_vma=False,
    )
```

profile of v0, /device:TPU:0, one launch (start us, length us, event | category | flops | bytes accessed | tf_op | source)
XLA Modules:
  0.0 459.6 jit_solution(9899254692592612599)
XLA Ops:
  7.2 2.2 convert_reduce_fusion.1
  9.4 1.8 convolution_bitcast_fusion.4
  11.3 1.5 copy.193
  17.2 1.2 copy-done.8
  18.4 1.0 copy-done.7
  19.4 6.6 %fusion.4 = f32[3,256,1,16,128]{1,4,3,0,2:T(8,128)S(1)} fusion(bf16[1,9,1,128,16,128]{3,5,1,4,0,2:T(8,128)(2,1)S(1)} %bitcast.390, bf16[1,9,1,128,16,128]{3,5,1,4,0,2:T(8,128)(2,1)S(1)} %bitcast.388, bf16[1,9,1,128,16,128]{3,5,1,4,0,2:T(8,128)(2,1)} %bitcast.392, bf16[3,9,128,256]{3,2,1,0:T(8,128)(2,1)S(1)} %copy-done), kind=kOutput, calls=%fused_computation.28 | convolution fusion | flops 3638034432 | bytes 22216704 | tf_op jit(solution)/shard_map/rtnchw,rtco->ronhw/dot_general | solution.py:56
  26.0 4.2 pad_maximum_fusion
  30.2 10.3 %copy.215 = f32[4,256,1,16,128]{4,3,2,0,1:T(8,128)} copy(f32[4,256,1,16,128]{1,4,3,0,2:T(8,128)} %pad_maximum_fusion) | data formatting | bytes 16777216 | tf_op jit(solution)/shard_map/concatenate | solution.py:59
  40.6 0.6 copy-done.10
  41.2 28.6 %reduce-scatter.10.cloned.1.call-done = f32[16,1]{1,0:T(8,128)} async-done(((f32[256,1]{1,0:T(8,128)}), f32[16,1]{1,0:T(8,128)}) %reduce-scatter.10.cloned.1.call-update) | async-done | bytes 80
  69.8 0.8 copy.248
  70.7 106.9 %reduce-scatter.6.cloned.1.call-done = f32[4,16,1,16,128]{4,3,2,0,1:T(8,128)} async-done(((f32[4,256,1,16,128]{4,3,2,0,1:T(8,128)}), f32[4,16,1,16,128]{4,3,2,0,1:T(8,128)}) %reduce-scatter.6.cloned.1.call-update) | async-done | bytes 524304 | tf_op jit(solution)/shard_map/reduce_scatter | solution.py:62
  177.7 1.3 fusion.106
  179.2 4.9 %all-reduce.25 = (f32[4,16]{1,0:T(4,128)S(1)}, f32[4,16]{1,0:T(4,128)S(1)}) all-reduce(f32[4,16]{1,0:T(4,128)S(1)} %copy.218, f32[4,16]{1,0:T(4,128)S(1)} %copy.216), channel_id=1, replica_groups=mesh['dp'=2,'chan'=16] {'dp'}, use_global_device_ids=true, to_apply=%region_4.5 | all-reduce | flops 128 | bytes 1024 | tf_op jit(solution)/shard_map/psum | solution.py:65
  184.1 3.1 fusion.5
  187.2 3.1 copy.219
  190.4 61.4 %reduce-scatter.8.cloned.1.call-done = f32[16,1,16,128]{3,2,1,0:T(8,128)} async-done(((f32[256,1,16,128]{3,2,1,0:T(8,128)}), f32[16,1,16,128]{3,2,1,0:T(8,128)}) %reduce-scatter.8.cloned.1.call-update) | async-done | bytes 131088 | tf_op jit(solution)/shard_map/reduce_scatter | solution.py:79
  251.8 1.1 fusion.108
  252.9 4.9 %all-reduce.24 = (f32[16]{0:T(128)S(1)}, f32[16]{0:T(128)S(1)}) all-reduce(f32[16]{0:T(128)S(1)} %get-tuple-element.55, f32[16]{0:T(128)S(1)} %get-tuple-element.54), channel_id=1, replica_groups=mesh['dp'=2,'chan'=16] {'dp'}, use_global_device_ids=true, to_apply=%region_11.12 | all-reduce | flops 32 | bytes 256 | tf_op jit(solution)/shard_map/psum | solution.py:82
  257.9 1.9 fusion.107
  259.8 4.9 %all-reduce.23 = (f32[16]{0:T(128)S(1)}, f32[16]{0:T(128)S(1)}) all-reduce(f32[16]{0:T(128)S(1)} %get-tuple-element.53, f32[16]{0:T(128)S(1)} %get-tuple-element.52), channel_id=1, replica_groups=mesh['dp'=2,'chan'=16] {'dp'}, use_global_device_ids=true, to_apply=%region_15.16 | all-reduce | flops 32 | bytes 256 | tf_op jit(solution)/shard_map/psum | solution.py:93
  264.7 1.7 multiply_convert_fusion.3
  266.4 37.0 %all-gather.3.cloned.1.call-done = bf16[256,1,16,128]{3,2,1,0:T(8,128)(2,1)} async-done(((bf16[16,1,16,128]{3,2,1,0:T(8,128)(2,1)}), bf16[256,1,16,128]{3,2,1,0:T(8,128)(2,1)}) %all-gather.3.cloned.1.call-update) | async-done | bytes 1048592 | tf_op jit(solution)/shard_map/all_gather | solution.py:103
  303.5 1.9 fusion.105
  305.4 5.1 %all-reduce.22 = (f32[4,16]{1,0:T(4,128)S(1)}, f32[4,16]{1,0:T(4,128)S(1)}) all-reduce(f32[4,16]{1,0:T(4,128)S(1)} %get-tuple-element.49, f32[4,16]{1,0:T(4,128)S(1)} %get-tuple-element.48), channel_id=1, replica_groups=mesh['dp'=2,'chan'=16] {'dp'}, use_global_device_ids=true, to_apply=%region_19.20 | all-reduce | flops 128 | bytes 1024 | tf_op jit(solution)/shard_map/psum | solution.py:119
  310.9 0.9 copy.221
  313.3 2.3 convert_reduce_fusion
  315.6 0.8 fusion.38
  316.6 31.2 %all-reduce.21 = bf16[256]{0:T(256)(128)(2,1)S(1)} all-reduce(bf16[256]{0:T(256)(128)(2,1)S(1)} %dynamic-update-slice), channel_id=1, replica_groups=mesh['dp'=2,'chan'=16] {'chan'}, use_global_device_ids=true, to_apply=%add.21 | all-reduce | flops 256 | bytes 1024 | tf_op jit(solution)/shard_map/reshape.60
  347.9 1.8 fusion.35
  349.8 8.4 %psum.95 = bf16[5,16,256]{2,1,0:T(8,128)(2,1)S(1)} all-reduce(bf16[5,16,256]{2,1,0:T(8,128)(2,1)S(1)} %pad_maximum_fusion.1), channel_id=1, replica_groups=mesh['dp'=2,'chan'=16] {'dp'}, use_global_device_ids=true, to_apply=%region_24.25 | all-reduce | flops 20480 | bytes 81920 | tf_op jit(solution)/shard_map/psum | solution.py:168
  358.1 0.6 convert_element_type.135
  360.1 0.7 multiply_convert_fusion.2
  360.8 0.9 all-gather.5.cloned.1.call-done
  361.7 4.1 slice.285
  365.8 5.0 %copy.250 = bf16[3,256,1,16,128]{1,4,3,0,2:T(8,128)(2,1)} copy(bf16[3,256,1,16,128]{4,3,2,0,1:T(8,128)(2,1)} %slice.285) | data formatting | bytes 6291456
  370.7 10.3 %bitcast_convert_fusion = bf16[3,9,128,256]{3,2,1,0:T(8,128)(2,1)} fusion(bf16[3,256,1,16,128]{1,4,3,0,2:T(8,128)(2,1)} %copy.250, bf16[1,9,1,128,16,128]{3,5,1,4,0,2:T(8,128)(2,1)} %bitcast.391, bf16[1,9,1,128,16,128]{3,5,1,4,0,2:T(8,128)(2,1)} %bitcast.389, bf16[1,9,1,128,16,128]{3,5,1,4,0,2:T(8,128)(2,1)} %bitcast.393), kind=kOutput, calls=%fused_computation.15 | convolution fusion | flops 3638919168 | bytes 19070976 | tf_op jit(solution)/shard_map/rtnchw,ronhw->rtco/dot_general | solution.py:143
  381.1 2.4 slice.284
  383.5 2.4 copy.249
  385.9 2.3 fusion.34
  388.3 13.2 %convolution_bitcast_fusion = f32[3,9,1,128,16,128]{3,5,4,2,1,0:T(8,128)} fusion(bf16[3,256,1,16,128]{1,4,3,0,2:T(8,128)(2,1)} %copy.250, bf16[3,9,128,256]{3,2,1,0:T(8,128)(2,1)S(1)} %copy-done), kind=kOutput, calls=%fused_computation.1 | convolution fusion | flops 3623878656 | bytes 33226752 | tf_op jit(solution)/shard_map/rtco,ronhw->rtnchw/dot_general | solution.py:135
  401.4 8.9 %slice_bitcast_fusion = (f32[1,128,16,128]{1,3,2,0:T(8,128)S(1)}, f32[1,128,16,128]{1,3,2,0:T(8,128)S(1)}, f32[1,128,16,128]{1,3,2,0:T(8,128)S(1)}, f32[1,128,16...) fusion(f32[3,9,1,128,16,128]{3,5,4,2,1,0:T(8,128)} %convolution, ...), kind=kLoop, calls=%fused_computation.88 | loop fusion | bytes 37748736 | tf_op jit(solution)/shard_map/squeeze | solution.py:161
  410.4 5.1 %fusion.31 = f32[1,128,16,128]{1,3,2,0:T(8,128)} fusion(f32[1,128,16,128]{1,3,2,0:T(8,128)} %get-tuple-element.87, f32[1,128,16,128]{1,3,2,0:T(8,128)} %get-tuple-element.86, f32[1,128,16,128]{1,3,2,0:T(8,128)S(1)} %get-tuple-element.85, f32[1,128,16,128]{1,3,2,0:T(8,128)S(1)} %get-tuple-element.84, f32[1,128,16,128]{1,3,2,0:T(8,128)S(1)} %get-tuple-element.83, ...), kind=kOutput, calls=%fused_computation.73 | convolution fusion | flops 139984896 | bytes 24183296 | tf_op jit(solution)/shard_map/co,onhw->nchw/dot_general | solution.py:132
  415.5 2.6 copy.229
  418.1 27.8 %all-reduce.29.cloned.1.call-done = (bf16[128,256]{0,1:T(8,128)(2,1)}, bf16[3,9,128,256]{3,2,1,0:T(8,128)(2,1)}, bf16[128,256]{1,0:T(8,128)(2,1)}) async-done(((bf16[128,256]{0,1:T(8,128)(2,1)}, bf16[3,9,128,256]{3,2,1,0:T(8,128)(2,1)}, bf16[128,256]{1,0:T(8,128)(2,1)}), (bf16[128,256]{0,1:T(8,128)(2,1)}, bf16[3,9,128,256]{3,2,1,0:T(8,128)(2,1)}, bf16[128,256]{1,0:T(8,128)(2,1)})) %all-reduce.29.cloned.1.call-update) | async-done | bytes 1900560 | tf_op jit(solution)/shard_map/psum | solution.py:165
  446.0 1.6 copy.230
  447.6 1.5 convert_element_type.134
  449.1 3.7 convert_element_type.132
  (80 shorter events, 7.8 us)
Async XLA Ops:
  7.2 12.2 %copy-start = (bf16[3,9,128,256]{3,2,1,0:T(8,128)(2,1)S(1)}, bf16[3,9,128,256]{3,2,1,0:T(8,128)(2,1)}, u32[]{:S(2)}) copy-start(bf16[3,9,128,256]{3,2,1,0:T(8,128)(2,1)} %param.10) | copy-start | bytes 5308420
  7.2 62.6 %reduce-scatter.10.cloned.1.call-start = ((), (), s32[]{:S(2)}) async-start(), calls=%async_computation.7 | async-start | bytes 139264
  11.2 166.5 %reduce-scatter.6.cloned.1.call-start = ((), (), s32[]{:S(2)}) async-start(), calls=%async_computation.3 | async-start | bytes 8912896 | tf_op jit(solution)/shard_map/reduce_scatter | solution.py:62
  14.8 1.9 copy-start.1
  14.8 1.9 copy-start.3
  15.4 3.0 copy-start.8
  16.2 9.8 %copy-start.6 = (bf16[9,1,128,16,128]{2,4,0,3,1:T(8,128)(2,1)}, bf16[9,1,128,16,128]{2,4,0,3,1:T(8,128)(2,1)S(1)}, u32[]{:S(2)}) copy-start(bf16[9,1,128,16,128]{2,4,0,3,1:T(8,128)(2,1)S(1)} %get-tuple-element.96) | copy-start | bytes 14155780
  16.7 2.7 copy-start.7
  40.5 0.7 copy-start.10
  40.5 30.1 %copy-start.11 = (bf16[5,16,256]{2,1,0:T(8,128)(2,1)S(1)}, bf16[5,16,256]{2,1,0:T(8,128)(2,1)}, u32[]{:S(2)}) copy-start(bf16[5,16,256]{2,1,0:T(8,128)(2,1)} %param.12) | copy-start | bytes 122884
  40.5 143.5 %copy-start.9 = (f32[5,16]{1,0:T(8,128)S(1)}, f32[5,16]{1,0:T(8,128)}, u32[]{:S(2)}) copy-start(f32[5,16]{1,0:T(8,128)} %param.13) | copy-start | bytes 964
  40.6 211.3 %reduce-scatter.8.cloned.1.call-start = ((), (), s32[]{:S(2)}) async-start(), calls=%async_computation.4 | async-start | bytes 2228224 | tf_op jit(solution)/shard_map/reduce_scatter | solution.py:79
  179.0 78.9 %copy-start.5 = (bf16[1,16,16,128]{3,2,1,0:T(8,128)(2,1)S(1)}, bf16[1,16,16,128]{3,2,1,0:T(8,128)(2,1)}, u32[]{:S(2)}) copy-start(bf16[1,16,16,128]{3,2,1,0:T(8,128)(2,1)} %param.15) | copy-start | bytes 196612
  184.1 119.4 %copy-start.2 = (f32[4,16,1,16,128]{4,3,2,0,1:T(8,128)S(1)}, f32[4,16,1,16,128]{4,3,2,0,1:T(8,128)}, u32[]{:S(2)}) copy-start(f32[4,16,1,16,128]{4,3,2,0,1:T(8,128)} %reduce-scatter.6.cloned.1.call-done) | copy-start | bytes 1572868
  190.3 121.7 %copy-start.12 = (u32[32]{0:T(128)S(1)}, u32[32]{0:T(128)}, u32[]{:S(2)}) copy-start(u32[32]{0:T(128)} %constant.80) | copy-start | bytes 388
  190.3 113.1 %all-gather.3.cloned.1.call-start = ((), (), s32[]{:S(2)}) async-start(), calls=%async_computation.5 | async-start | bytes 1114112 | tf_op jit(solution)/shard_map/all_gather | solution.py:103
  266.4 95.3 %all-gather.5.cloned.1.call-start = ((), (), s32[]{:S(2)}) async-start(), calls=%async_computation.6 | async-start | bytes 4456448 | tf_op jit(solution)/shard_map/all_gather | solution.py:129
  305.4 54.6 %copy-start.4 = (bf16[128,256]{1,0:T(8,128)(2,1)S(1)}, bf16[128,256]{1,0:T(8,128)(2,1)}, u32[]{:S(2)}) copy-start(bf16[128,256]{1,0:T(8,128)(2,1)} %param.11) | copy-start | bytes 196612
  311.8 134.1 %all-reduce.29.cloned.1.call-start = ((), (), s32[]{:S(2)}) async-start(), calls=%async_computation.8 | async-start | bytes 3801088 | tf_op jit(solution)/shard_map/psum | solution.py:165
Sparse Core Ops, SparseCore 0:
  12.0 57.7 reduce-scatter.9
  73.9 103.7 reduce-scatter.5
  190.5 61.3 reduce-scatter.7
  266.5 36.8 all-gather.2
  311.9 49.7 all-gather.4
  388.4 57.5 all-reduce.28
where the time goes:
time: 461 us; the launch traced here: 460 us
  waiting for transfers between devices  263 us (57%)
  blocking collectives  59.4 us (13%)
  local copies, waits for them, and re-layouts  51.1 us (11%)
  matrix products  47.7 us (10%)
  other arithmetic  23 us (5%)
  between operations  15.1 us (3%)
    reduce_scatter x1, waiting for transfers between devices, local(): lax.psum_scatter(spatial_term, 'chan', scatter_dimension=1, tiled=True)  107 us
    reduce_scatter x1, waiting for transfers between devices, local(): lax.psum_scatter(spatial + pool_part[:, :, None, None], 'chan', scatter_d...  61.4 us
    all_gather x1, waiting for transfers between devices, local(): portion = lax.all_gather(proj_low, 'chan', axis=0, tiled=True)  37 us
    another operation x1, blocking collectives  31.2 us
    unnamed x7, waiting for transfers between devices  28.7 us
    psum x1, waiting for transfers between devices, local(): lax.psum(one_grad.astype(jnp.bfloat16), 'dp').astype(jnp.float32)  27.8 us
    unnamed x53, local copies, waits for them, and re-layouts  20.4 us
    dot_general x1, matrix products, local(): jnp.einsum('rtco,ronhw->rtnchw', w_atrous, spatial_portion[1:], preferred...  13.2 us
  transfers between devices with their start and end apart: 6, of which 6 were waited for; matrix products, arithmetic and copies ran while one was open for 14% of the time, Pallas kernels for 0%

commit v1 on v0

--- a/solution.py
+++ b/solution.py
@@ -1,6 +1,10 @@
+import functools
+
 import jax
 import jax.numpy as jnp
 from jax import lax
+from jax.experimental import pallas as pl
+from jax.experimental.pallas import tpu as pltpu
 from jax.sharding import PartitionSpec as P
 
 atrous_rates = (6, 12, 18)
@@ -181,6 +185,796 @@
     )
 
 
+MESH = pl.DeviceIdType.MESH
+F32 = jnp.float32
+BF16 = jnp.bfloat16
+ROWS = 16
+COLS = 128
+PIXELS = ROWS * COLS
+WIDE = PIXELS + 128
+CIN_PART = 128
+COUT = 256
+GROUPS = 8
+BLOCK = 256
+ORDER = (0, 3, 2, 1)
+
+
+def branch_rows(branch):
+    if branch == 0:
+        return [(None, 0)]
+    rate = atrous_rates[branch - 1]
+    return [(i, (i - 1) * rate) for i in (1, 0, 2) if abs((i - 1) * rate) < ROWS]
+
+
+def weight_slots():
+    slots = {}
+    count = 0
+    spans = {}
+    for branch in ORDER:
+        begin = count
+        for i, _ in branch_rows(branch):
+            slots[(branch, i)] = count
+            count += 1 if branch == 0 else 3
+        if branch == 0:
+            slots["pool"] = count
+            count += 1
+        spans[branch] = (begin, count)
+    return slots, spans, count
+
+
+SLOTS, SPANS, NSLOTS = weight_slots()
+
+
+def width_of(branch):
+    return WIDE if branch == 0 else PIXELS
+
+
+def dot(a, b):
+    return jnp.dot(a, b, preferred_element_type=F32)
+
+
+def dot_nt(a, b):
+    return lax.dot_general(a, b, (((1,), (1,)), ((), ())), preferred_element_type=F32)
+
+
+def iota(shape, dim):
+    return lax.broadcasted_iota(jnp.int32, shape, dim)
+
+
+def lane_sum(v):
+    return jnp.sum(v, axis=1, keepdims=True)
+
+
+def split_lanes(column, lanes=(0, 1, 2)):
+    high = column.astype(BF16).astype(F32)
+    mid = (column - high).astype(BF16).astype(F32)
+    low = column - high - mid
+    lane = iota((column.shape[0], 128), 1)
+    out = jnp.where(lane == lanes[0], high, 0.0)
+    out = out + jnp.where(lane == lanes[1], mid, 0.0)
+    return out + jnp.where(lane == lanes[2], low, 0.0)
+
+
+def encode_pair(v):
+    lane = iota(v.shape, v.ndim - 1)
+    high = v.astype(BF16).astype(F32)
+    low = v - high
+    return jnp.where(lane == 0, high, jnp.where(lane == 1, low, 0.0)).astype(BF16)
+
+
+def decode_pair(e):
+    return jnp.broadcast_to(jnp.sum(e.astype(F32), axis=-1, keepdims=True), e.shape)
+
+
+def shift_cols(v, by):
+    if by == 0:
+        return v
+    lane = iota((v.shape[0], 128), 1)
+    keep = (lane >= by) if by > 0 else (lane < 128 + by)
+    parts = []
+    for h in range(v.shape[1] // 128):
+        tile = v[:, h * 128 : (h + 1) * 128]
+        parts.append(jnp.where(keep, pltpu.roll(tile, by % 128, 1), 0.0))
+    return jnp.concatenate(parts, axis=1) if len(parts) > 1 else parts[0]
+
+
+def sigmoid(z):
+    return 0.5 * jnp.tanh(0.5 * z) + 0.5
+
+
+INPUTS = ("feat", "og", "w1", "wa", "wpool", "wproj", "par")
+OUTPUTS = ("out", "fg", "dw1", "dwa", "dwpool", "dwproj", "dpar")
+
+
+def scratch_table(sems):
+    vm = pltpu.VMEM
+    return {
+        "fsib": vm((2048, 128), BF16),
+        "foth": vm((2048, 128), BF16),
+        "x": vm((256, PIXELS), BF16),
+        "tw": vm((NSLOTS, GROUPS, 2, 16, 128), BF16),
+        "lw": vm((NSLOTS, GROUPS, 16, 256), BF16),
+        "acc": vm((4, GROUPS, 16, PIXELS), F32),
+        "acp": vm((GROUPS, 16, 128), F32),
+        "ys": vm((4, 4, 16, WIDE), BF16),
+        "yr": vm((4, 4, 16, WIDE), BF16),
+        "zs": vm((4, 4, 16, WIDE), BF16),
+        "zr": vm((4, 4, 16, WIDE), BF16),
+        "g": vm((4, 2, GROUPS, 16, WIDE), BF16),
+        "ogs": vm((2, GROUPS, 16, PIXELS), BF16),
+        "pt": vm((GROUPS, 16, 128), F32),
+        "wp": vm((GROUPS, 5, 16, 256), BF16),
+        "wpt": vm((256, 640), BF16),
+        "xs": vm((2, 3, 3, 128, PIXELS), BF16),
+        "act": vm((2, 4, GROUPS, 16, PIXELS), BF16),
+        "ao": vm((2, 4, 16, PIXELS), BF16),
+        "pa": vm((5, 128, 128), F32),
+        "pb": vm((5, 128, 128), F32),
+        "pm": vm((5, 128, 128), F32),
+        "pi": vm((5, 128, 128), F32),
+        "s1": vm((5, 128, 128), F32),
+        "s2": vm((5, 128, 128), F32),
+        "pr": vm((2, GROUPS, 16, PIXELS), F32),
+        "dzp": vm((2, GROUPS, 16, PIXELS), F32),
+        "dp": vm((2, GROUPS, 2, 16, PIXELS), BF16),
+        "dpo": vm((GROUPS, 2, 16, 128), BF16),
+        "d": vm((4, 2, GROUPS, 2, 16, PIXELS), BF16),
+        "fga": vm((128, PIXELS), F32),
+        "pooled": vm((2, 128, 128), F32),
+        "ppool": vm((2, 128, 128), F32),
+        "ss": pltpu.SemaphoreType.DMA((sems,)),
+        "rs": pltpu.SemaphoreType.DMA((sems,)),
+    }
+
+
+class Refs:
+    pass
+
+
+NSEMS = 160
+
+
+def head_kernel(*refs):
+    names = INPUTS + OUTPUTS + tuple(scratch_table(NSEMS))
+    r = Refs()
+    for name, ref in zip(names, refs, strict=True):
+        setattr(r, name, ref)
+    x = lax.axis_index("dp")
+    c = lax.axis_index("chan")
+    k = lax.rem(c, 2)
+    y = lax.rem(lax.div(c, 2), 2)
+    z = lax.div(c, 4)
+
+    def dev(xx, zz, yy, kk):
+        return {"dp": xx, "chan": (zz * 2 + yy) * 2 + kk}
+
+    sibling = dev(x, z, y, 1 - k)
+    xdev = dev(1 - x, z, y, k)
+    ydev = dev(x, z, 1 - y, k)
+    zpos = [None] + [lax.rem(z + i, 4) for i in (1, 2, 3)]
+    zfrom = [None] + [lax.rem(z + 4 - i, 4) for i in (1, 2, 3)]
+    zdev = [None] + [dev(x, zpos[i], y, k) for i in (1, 2, 3)]
+
+    counter = [0]
+    sent = []
+
+    def new(n=1):
+        first = counter[0]
+        counter[0] += n
+        assert counter[0] <= NSEMS
+        return first
+
+    def rcopy(src, dst, n, device):
+        return pltpu.make_async_remote_copy(
+            src_ref=src,
+            dst_ref=dst,
+            send_sem=r.ss.at[n],
+            recv_sem=r.rs.at[n],
+            device_id=device,
+            device_id_type=MESH,
+        )
+
+    def send(src, dst, n, device, group=None):
+        copy = rcopy(src, dst, n, device)
+        copy.start()
+        (sent if group is None else group).append(copy)
+
+    def arrived(ref, n, device):
+        rcopy(ref, ref, n, device).wait_recv()
+
+    barrier = pltpu.get_barrier_semaphore()
+    partners = [sibling, xdev, ydev] + zdev[1:]
+    for partner in partners:
+        pl.semaphore_signal(barrier, inc=1, device_id=partner, device_id_type=MESH)
+    pl.semaphore_wait(barrier, len(partners))
+
+    n_feat = new()
+    send(r.feat, r.fsib, n_feat, sibling)
+
+    rr = iota((256, 256), 0)
+    cc = iota((256, 256), 1)
+    perm = jnp.where(cc == lax.rem(rr, 16) * 16 + lax.div(rr, 16), 1.0, 0.0).astype(BF16)
+    eye = jnp.where(rr == cc, 1.0, 0.0).astype(BF16)
+
+    def permuted(ref, block):
+        return dot(perm, ref[block * 256 : (block + 1) * 256, :]).astype(BF16)
+
+    def pre_group(yy, zz):
+        return yy * 4 + zz
+
+    def own_group(yy, zz):
+        return zz * 2 + yy
+
+    class Gather:
+        def __init__(self, slot, group, across):
+            self.slot, self.group, self.across = slot, group, across
+            self.nz, self.ny, self.nx = new(3), new(4), new(8) if across else None
+
+        def start(self):
+            mine = self.slot(self.group(y, z))
+            for i in (1, 2, 3):
+                send(mine, mine, self.nz + i - 1, zdev[i])
+            send(mine, mine, self.ny, ydev)
+            if self.across:
+                send(mine, mine, self.nx, xdev)
+
+        def forward_z(self):
+            for i in (1, 2, 3):
+                ref = self.slot(self.group(y, zfrom[i]))
+                arrived(ref, self.nz + i - 1, zdev[i])
+                send(ref, ref, self.ny + i, ydev)
+                if self.across:
+                    send(ref, ref, self.nx + i, xdev)
+
+        def forward_y(self):
+            for i in range(4):
+                ref = self.slot(self.group(1 - y, z if i == 0 else zfrom[i]))
+                arrived(ref, self.ny + i, ydev)
+                if self.across:
+                    send(ref, ref, self.nx + 4 + i, xdev)
+
+        def finish(self, other):
+            if self.across:
+                for i in range(8):
+                    yy = y if i < 4 else 1 - y
+                    zz = z if i % 4 == 0 else zfrom[i % 4]
+                    arrived(other(self.group(yy, zz)), self.nx + i, xdev)
+
+    g_og = Gather(lambda g: r.ogs.at[x, g], own_group, True)
+    g_par = Gather(lambda g: r.pt.at[g], own_group, False)
+    g_wp = Gather(lambda g: r.wp.at[g], own_group, False)
+    g_pre = {}
+    for b in ORDER:
+        w = width_of(b)
+        g_pre[b] = Gather(lambda g, b=b, w=w: r.g.at[b, x, g, :, pl.ds(0, w)], pre_group, True)
+
+    mine = own_group(y, z)
+    og = permuted(r.og, 0)
+    for h in range(ROWS):
+        r.ogs[x, mine, :, h * 128 : (h + 1) * 128] = og[h * 16 : (h + 1) * 16]
+    r.pt[mine] = r.par[...]
+    r.wp[mine] = r.wproj[...]
+
+    n_w = {b: new() for b in ORDER}
+
+    def weight_ref(b, i, j):
+        return r.w1 if b == 0 else r.wa.at[(b - 1) * 9 + 3 * i + j]
+
+    def transpose_into(slot, ref):
+        t = dot_nt(eye, ref[...]).astype(BF16)
+        r.tw[slot] = t.reshape(GROUPS, 2, 16, 128)
+        r.lw[slot, :, :, 0:128] = r.tw[slot, :, k]
+
+    def prepare_weights(b):
+        for i, _ in branch_rows(b):
+            slot = SLOTS[(b, i)]
+            if b == 0:
+                transpose_into(slot, r.w1)
+                transpose_into(SLOTS["pool"], r.wpool)
+            else:
+                for j in range(3):
+                    transpose_into(slot + j, weight_ref(b, i, j))
+        lo, hi = SPANS[b]
+        send(
+            r.tw.at[pl.ds(lo, hi - lo), :, 1 - k],
+            r.lw.at[pl.ds(lo, hi - lo), :, :, pl.ds(128, 128)],
+            n_w[b],
+            sibling,
+        )
+
+    def wait_weights(b):
+        lo, hi = SPANS[b]
+        arrived(r.lw.at[pl.ds(lo, hi - lo), :, :, pl.ds(128, 128)], n_w[b], sibling)
+
+    prepare_weights(0)
+
+    def place(ref, base):
+        for block in range(8):
+            t = permuted(ref, block)
+            for h in range(ROWS):
+                r.x[base + block * 16 : base + (block + 1) * 16, h * 128 : (h + 1) * 128] = t[
+                    h * 16 : (h + 1) * 16
+                ]
+
+    place(r.feat, 0)
+    arrived(r.fsib, n_feat, sibling)
+    place(r.fsib, 128)
+
+    def convolve(b):
+        for q in range(PIXELS // BLOCK):
+            px = slice(q * BLOCK, (q + 1) * BLOCK)
+            total = None
+            for i, offset in branch_rows(b):
+                source = q + offset * COLS // BLOCK
+                if source < 0 or source >= PIXELS // BLOCK:
+                    continue
+                slot = SLOTS[(b, i)]
+                count = 1 if b == 0 else 3
+                weights = r.lw[slot : slot + count].reshape(count * 128, 256)
+                part = dot(weights, r.x[:, source * BLOCK : (source + 1) * BLOCK])
+                total = part if total is None else total + part
+            if b:
+                rate = atrous_rates[b - 1]
+                total = (
+                    total[128:256]
+                    + shift_cols(total[0:128], rate)
+                    + shift_cols(total[256:384], -rate)
+                )
+            r.acc[b, :, :, px] = total.reshape(GROUPS, 16, BLOCK)
+        if b == 0:
+            pooled = jnp.zeros((256, 128), F32)
+            for h in range(ROWS):
+                pooled = pooled + r.x[:, h * 128 : (h + 1) * 128].astype(F32)
+            column = lane_sum(pooled) / PIXELS
+            r.pooled[x] = jnp.broadcast_to(column[0:128], (128, 128))
+            terms = split_lanes(column).astype(BF16)
+            slot = SLOTS["pool"]
+            sums = lane_sum(dot(r.lw[slot].reshape(128, 256), terms))
+            r.acp[...] = jnp.broadcast_to(sums, (128, 128)).reshape(GROUPS, 16, 128)
+
+    n_ry = {b: new() for b in ORDER}
+    n_rz = {b: new(3) for b in ORDER}
+
+    def reduce_y_send(b):
+        w = width_of(b)
+        r.ys[b, :, :, 0:PIXELS] = r.acc[b, pl.ds(4 * (1 - y), 4)].astype(BF16)
+        if b == 0:
+            r.ys[b, :, :, PIXELS:WIDE] = encode_pair(r.acp[pl.ds(4 * (1 - y), 4)])
+        send(r.ys.at[b, :, :, pl.ds(0, w)], r.yr.at[b, :, :, pl.ds(0, w)], n_ry[b], ydev)
+
+    def reduce_z_send(b):
+        w = width_of(b)
+        arrived(r.yr.at[b, :, :, pl.ds(0, w)], n_ry[b], ydev)
+        for i in (1, 2, 3, 0):
+            zz = z if i == 0 else zpos[i]
+            g = 4 * y + zz
+            s = r.acc[b, g] + r.yr[b, zz, :, 0:PIXELS].astype(F32)
+            if b == 0:
+                e = r.acp[g] + decode_pair(r.yr[b, zz, :, PIXELS:WIDE])
+            if i == 0:
+                r.acc[b, g] = s
+                if b == 0:
+                    r.acp[g] = e
+            else:
+                r.zs[b, i, :, 0:PIXELS] = s.astype(BF16)
+                if b == 0:
+                    r.zs[b, i, :, PIXELS:WIDE] = encode_pair(e)
+                send(
+                    r.zs.at[b, i, :, pl.ds(0, w)],
+                    r.zr.at[b, i, :, pl.ds(0, w)],
+                    n_rz[b] + i - 1,
+                    zdev[i],
+                )
+
+    def reduce_finish(b):
+        w = width_of(b)
+        g = pre_group(y, z)
+        total = r.acc[b, g]
+        extra = r.acp[g] if b == 0 else None
+        for i in (1, 2, 3):
+            arrived(r.zr.at[b, i, :, pl.ds(0, w)], n_rz[b] + i - 1, zdev[i])
+            total = total + r.zr[b, i, :, 0:PIXELS].astype(F32)
+            if b == 0:
+                extra = extra + decode_pair(r.zr[b, i, :, PIXELS:WIDE])
+        r.g[b, x, g, :, 0:PIXELS] = total.astype(BF16)
+        if b == 0:
+            r.g[b, x, g, :, PIXELS:WIDE] = encode_pair(extra)
+        g_pre[b].start()
+
+    def other_pre(b):
+        w = width_of(b)
+        return lambda g: r.g.at[b, 1 - x, g, :, pl.ds(0, w)]
+
+    shift_pairs = []
+    lane_r = iota((128, 128), 0)
+    lane_c = iota((128, 128), 1)
+    for rate in atrous_rates:
+        left = jnp.where(lane_r == lane_c - rate, 1.0, 0.0).astype(BF16)
+        right = jnp.where(lane_r == lane_c + rate, 1.0, 0.0).astype(BF16)
+        shift_pairs.append(jnp.concatenate([left, right], axis=1))
+
+    def place_shifted(ref, image):
+        for block in range(8):
+            t = permuted(ref, block)
+            rows = slice(block * 16, (block + 1) * 16)
+            for a in range(3):
+                both = dot(t, shift_pairs[a]).astype(BF16)
+                for h in range(ROWS):
+                    px = slice(h * 128, (h + 1) * 128)
+                    hc = slice(h * 16, (h + 1) * 16)
+                    r.xs[image, a, 0, rows, px] = both[hc, 0:128]
+                    r.xs[image, a, 1, rows, px] = t[hc]
+                    r.xs[image, a, 2, rows, px] = both[hc, 128:256]
+
+    n_foth = new()
+
+    count = float(2 * PIXELS)
+
+    def finish_norm(b, rows, s, q, gain, bias):
+        mean = lane_sum(s) / count
+        inv = lax.rsqrt(lane_sum(q) / count - mean * mean + norm_eps)
+        scale = gain * inv
+        r.pa[b, rows] = jnp.broadcast_to(scale, (16, 128))
+        r.pb[b, rows] = jnp.broadcast_to(bias - mean * scale, (16, 128))
+        r.pm[b, rows] = jnp.broadcast_to(mean, (16, 128))
+        r.pi[b, rows] = jnp.broadcast_to(inv, (16, 128))
+
+    def branch_norm(b):
+        def group(g, _):
+            rows = pl.ds(pl.multiple_of(g * 16, 16), 16)
+            s = jnp.zeros((16, 128), F32)
+            q = jnp.zeros((16, 128), F32)
+            for image in range(2):
+                for h in range(ROWS):
+                    v = r.g[b, image, g, :, h * 128 : (h + 1) * 128].astype(F32)
+                    s = s + v
+                    q = q + v * v
+            par = r.pt[g]
+            finish_norm(b, rows, s, q, par[:, b : b + 1], par[:, 8 + b : 9 + b])
+            scale, base = r.pa[b, rows], r.pb[b, rows]
+            for image in range(2):
+                for h in range(ROWS):
+                    px = slice(h * 128, (h + 1) * 128)
+                    zed = r.g[b, image, g, :, px].astype(F32) * scale + base
+                    r.act[image, b, g, :, px] = (zed * sigmoid(zed)).astype(BF16)
+            return 0
+
+        lax.fori_loop(0, GROUPS, group, 0)
+
+    g_par.start()
+    g_wp.start()
+    steps = len(ORDER)
+    for s in range(steps + 3):
+        if s < steps:
+            b = ORDER[s]
+            wait_weights(b)
+            convolve(b)
+            reduce_y_send(b)
+            if s + 1 < steps:
+                prepare_weights(ORDER[s + 1])
+        if s == 0:
+            g_og.start()
+        if 1 <= s <= steps:
+            reduce_z_send(ORDER[s - 1])
+        if s == 1:
+            g_par.forward_z()
+            g_wp.forward_z()
+            g_og.forward_z()
+        if s == 2:
+            g_par.forward_y()
+            g_wp.forward_y()
+        if 2 <= s <= steps + 1:
+            reduce_finish(ORDER[s - 2])
+        if s == 3:
+            place_shifted(r.feat, x)
+        if 3 <= s <= steps + 2:
+            g_pre[ORDER[s - 3]].forward_z()
+        if s >= 4:
+            g_pre[ORDER[s - 4]].forward_y()
+    g_pre[ORDER[steps - 1]].forward_y()
+    g_og.forward_y()
+    send(r.feat, r.foth, n_foth, xdev)
+
+    for b in range(5):
+        r.wpt[:, b * 128 : (b + 1) * 128] = dot_nt(eye, r.wp[:, b].reshape(128, 256)).astype(BF16)
+
+    for b in ORDER:
+        g_pre[b].finish(other_pre(b))
+        branch_norm(b)
+
+    pool_act = []
+    lane128 = iota((128, 128), 1)
+    pool_cols = jnp.zeros((128, 128), F32)
+    for image in range(2):
+        pre = decode_pair(r.g[0, image, :, :, PIXELS:WIDE]).reshape(128, 128)
+        r.ppool[image] = pre
+        pool_cols = pool_cols + jnp.where(lane128 == image, pre * sigmoid(pre), 0.0)
+    pool_cols = pool_cols.astype(BF16)
+    pool_out = dot(r.wpt[:, 512:640], pool_cols)
+
+    n_pp = new(2)
+    pp_sent = []
+    for image in range(2):
+        column = pool_out[:, image : image + 1]
+        for q in range(PIXELS // BLOCK):
+            px = slice(q * BLOCK, (q + 1) * BLOCK)
+            part = dot(r.wpt[:, 0:512], r.act[image, :, :, :, px].reshape(512, BLOCK)) + column
+            part = part.reshape(GROUPS, 2, 16, BLOCK)
+            r.acc[2 * image, :, :, px] = part[:, 0]
+            r.acc[2 * image + 1, :, :, px] = part[:, 1]
+        send(r.acc.at[2 * image + 1 - k], r.pr.at[image], n_pp + image, sibling, pp_sent)
+
+    for image in range(2):
+        for b in range(4):
+            r.ao[image, b] = r.act[image, b, mine]
+
+    g_og.finish(lambda g: r.ogs.at[1 - x, g])
+    for image in range(2):
+        arrived(r.pr.at[image], n_pp + image, sibling)
+
+    def proj_group(g, _):
+        rows = pl.ds(pl.multiple_of(g * 16, 16), 16)
+        s = jnp.zeros((16, 128), F32)
+        q = jnp.zeros((16, 128), F32)
+        for image in range(2):
+            for h in range(ROWS):
+                px = slice(h * 128, (h + 1) * 128)
+                v = r.acc[2 * image + k, g, :, px] + r.pr[image, g, :, px]
+                r.pr[image, g, :, px] = v
+                s = s + v
+                q = q + v * v
+        par = r.pt[g]
+        finish_norm(4, rows, s, q, par[:, 4:5], par[:, 12:13])
+        scale, base = r.pa[4, rows], r.pb[4, rows]
+        mean, inv = r.pm[4, rows], r.pi[4, rows]
+        s1 = jnp.zeros((16, 128), F32)
+        s2 = jnp.zeros((16, 128), F32)
+        for image in range(2):
+            for h in range(ROWS):
+                px = slice(h * 128, (h + 1) * 128)
+                v = r.pr[image, g, :, px]
+                zed = v * scale + base
+                sg = sigmoid(zed)
+                dz = r.ogs[image, g, :, px].astype(F32) * (sg * (1.0 + zed * (1.0 - sg)))
+                r.dzp[image, g, :, px] = dz
+                s1 = s1 + dz
+                s2 = s2 + dz * (v - mean)
+        s1 = jnp.broadcast_to(lane_sum(s1), (16, 128))
+        s2 = jnp.broadcast_to(lane_sum(s2), (16, 128)) * inv
+        r.s1[4, rows] = s1
+        r.s2[4, rows] = s2
+        c1 = -scale * s1 / count
+        c2 = -scale * inv * s2 / count
+        for image in range(2):
+            for h in range(ROWS):
+                px = slice(h * 128, (h + 1) * 128)
+                v = r.pr[image, g, :, px]
+                low = scale * r.dzp[image, g, :, px] + ((v - mean) * c2 + c1)
+                r.dp[image, g, k, :, px] = low.astype(BF16)
+        return 0
+
+    lax.fori_loop(0, GROUPS, proj_group, 0)
+
+    n_dp = new(2)
+    for image in range(2):
+        ref = r.dp.at[image, :, k]
+        send(ref, ref, n_dp + image, sibling)
+
+    my_rows = pl.ds(pl.multiple_of(mine * 16, 16), 16)
+    scale, base = r.pa[4, my_rows], r.pb[4, my_rows]
+    for h in range(ROWS):
+        zed = r.pr[x, mine, :, h * 128 : (h + 1) * 128] * scale + base
+        r.out[pl.ds(h, 16, stride=16), :] = zed * sigmoid(zed)
+
+    for image in range(2):
+        arrived(r.dp.at[image, :, 1 - k], n_dp + image, sibling)
+
+    ones = jnp.ones((PIXELS, 128), BF16)
+    wp4 = r.wp[:, 4].reshape(128, 256)
+    dpo = jnp.zeros((128, 128), F32)
+    dwp4 = jnp.zeros((16, 256), F32)
+    lane16 = iota((16, 128), 1)
+    for image in range(2):
+        dps = r.dp[image].reshape(256, PIXELS)
+        row_sums = dot(dps, ones)[:, 0:1]
+        pool_grad = lane_sum(dot(wp4, split_lanes(row_sums).astype(BF16)))
+        pre = r.ppool[image][:, 0:1]
+        sg = sigmoid(pre)
+        low = (pool_grad * (sg * (1.0 + pre * (1.0 - sg)))).astype(BF16).astype(F32)
+        for lane in (image, image + 2, image + 4):
+            dpo = dpo + jnp.where(lane128 == lane, low, 0.0)
+        mine_pre = r.ppool[image, my_rows][:, 0:1]
+        mine_act = (mine_pre * sigmoid(mine_pre)).astype(BF16).astype(F32)
+        dwp4 = dwp4 + mine_act * dot_nt(jnp.ones((16, PIXELS), BF16), dps)
+    r.dwproj[4] = dwp4
+    r.dpo[:, k] = dpo.astype(BF16).reshape(GROUPS, 16, 128)
+    n_dpo = new()
+    ref = r.dpo.at[:, k]
+    send(ref, ref, n_dpo, sibling)
+
+    dwp = jnp.zeros((64, 256), F32)
+    for image in range(2):
+        dwp = dwp + dot_nt(r.ao[image].reshape(64, PIXELS), r.dp[image].reshape(256, PIXELS))
+    r.dwproj[0:4] = dwp.reshape(4, 16, 256)
+
+    for copy in pp_sent:
+        copy.wait_send()
+    for image in range(2):
+        for q in range(PIXELS // BLOCK):
+            px = slice(q * BLOCK, (q + 1) * BLOCK)
+            dblock = r.dp[image, :, :, :, px].reshape(256, BLOCK)
+            for b in range(4):
+                part = dot(r.wp[:, b].reshape(128, 256), dblock)
+                r.acc[b, :, :, px] = part.reshape(GROUPS, 16, BLOCK)
+        for b in ORDER:
+
+            def slope_group(g, _, b=b, image=image):
+                rows = pl.ds(pl.multiple_of(g * 16, 16), 16)
+                scale, base, mean = r.pa[b, rows], r.pb[b, rows], r.pm[b, rows]
+                s1 = jnp.zeros((16, 128), F32)
+                s2 = jnp.zeros((16, 128), F32)
+                for h in range(ROWS):
+                    px = slice(h * 128, (h + 1) * 128)
+                    v = r.g[b, image, g, :, px].astype(F32)
+                    zed = v * scale + base
+                    sg = sigmoid(zed)
+                    dz = r.acc[b, g, :, px] * (sg * (1.0 + zed * (1.0 - sg)))
+                    s1 = s1 + dz
+                    s2 = s2 + dz * (v - mean)
+                    r.act[image, b, g, :, px] = dz.astype(BF16)
+                if image == 0:
+                    r.s1[b, rows] = s1
+                    r.s2[b, rows] = s2
+                else:
+                    r.s1[b, rows] = jnp.broadcast_to(lane_sum(r.s1[b, rows] + s1), (16, 128))
+                    r.s2[b, rows] = jnp.broadcast_to(lane_sum(r.s2[b, rows] + s2), (16, 128)) * (
+                        r.pi[b, rows]
+                    )
+                return 0
+
+            lax.fori_loop(0, GROUPS, slope_group, 0)
+
+    n_d = {b: new(2) for b in ORDER}
+    for b in ORDER:
+        for image in range(2):
+
+            def low_group(g, _, b=b, image=image):
+                rows = pl.ds(pl.multiple_of(g * 16, 16), 16)
+                scale, mean = r.pa[b, rows], r.pm[b, rows]
+                c1 = -scale * r.s1[b, rows] / count
+                c2 = -scale * r.pi[b, rows] * r.s2[b, rows] / count
+                for h in range(ROWS):
+                    px = slice(h * 128, (h + 1) * 128)
+                    v = r.g[b, image, g, :, px].astype(F32)
+                    low = scale * r.act[image, b, g, :, px].astype(F32) + ((v - mean) * c2 + c1)
+                    r.d[b, image, g, k, :, px] = low.astype(BF16)
+                return 0
+
+            lax.fori_loop(0, GROUPS, low_group, 0)
+            ref = r.d.at[b, image, :, k]
+            send(ref, ref, n_d[b] + image, sibling)
+
+    tile = jnp.zeros((16, 128), F32)
+    for b in range(5):
+        tile = tile + jnp.where(lane16 == b, r.s2[b, my_rows], 0.0)
+        tile = tile + jnp.where(lane16 == 8 + b, r.s1[b, my_rows], 0.0)
+    r.dpar[...] = tile
+
+    arrived(r.foth, n_foth, xdev)
+    place_shifted(r.foth, 1 - x)
+    pooled = jnp.zeros((128, 128), F32)
+    for h in range(ROWS):
+        pooled = pooled + r.xs[1 - x, 0, 1, :, h * 128 : (h + 1) * 128].astype(F32)
+    r.pooled[1 - x] = jnp.broadcast_to(lane_sum(pooled) / PIXELS, (128, 128))
+
+    arrived(r.dpo.at[:, 1 - k], n_dpo, sibling)
+    dpo = r.dpo[...].reshape(256, 128)
+    pooled = jnp.zeros((128, 128), F32)
+    for image in range(2):
+        pooled = pooled + split_lanes(r.pooled[image][:, 0:1], (image, image + 2, image + 4))
+    r.dwpool[...] = dot_nt(pooled.astype(BF16), dpo)
+    spread = dot(r.wpool[...], dpo)
+    fg_pool = lane_sum(jnp.where(lane128 == x, spread, 0.0)) / PIXELS
+
+    for b in ORDER:
+        for image in range(2):
+            arrived(r.d.at[b, image, :, 1 - k], n_d[b] + image, sibling)
+        if b == 0:
+            total = jnp.zeros((128, 256), F32)
+            for image in range(2):
+                total = total + dot_nt(r.xs[image, 0, 1], r.d[0, image].reshape(256, PIXELS))
+            r.dw1[...] = total
+        else:
+            met = dict(branch_rows(b))
+            for i in range(3):
+                where = pl.ds((b - 1) * 9 + 3 * i, 3)
+                if i not in met:
+                    r.dwa[where] = jnp.zeros((3, 128, 256), F32)
+                    continue
+                offset = met[i]
+                first, last = max(0, -offset), min(ROWS, ROWS - offset)
+                there = slice((first + offset) * 128, (last + offset) * 128)
+                here = slice(first * 128, last * 128)
+                total = jnp.zeros((384, 256), F32)
+                for image in range(2):
+                    total = total + dot_nt(
+                        r.xs[image, b - 1, :, :, there].reshape(384, (last - first) * 128),
+                        r.d[b, image, :, :, :, here].reshape(256, (last - first) * 128),
+                    )
+                r.dwa[where] = total.reshape(3, 128, 256)
+        for q in range(PIXELS // BLOCK):
+            px = slice(q * BLOCK, (q + 1) * BLOCK)
+            if b == 0:
+                part = dot(r.w1[...], r.d[0, x, :, :, :, px].reshape(256, BLOCK)) + fg_pool
+                r.fga[:, px] = part
+                continue
+            total = None
+            for i, offset in branch_rows(b):
+                source = q - offset * COLS // BLOCK
+                if source < 0 or source >= PIXELS // BLOCK:
+                    continue
+                weights = r.wa[pl.ds((b - 1) * 9 + 3 * i, 3)].reshape(384, 256)
+                dblock = r.d[b, x, :, :, :, source * BLOCK : (source + 1) * BLOCK]
+                part = dot(weights, dblock.reshape(256, BLOCK))
+                total = part if total is None else total + part
+            rate = atrous_rates[b - 1]
+            total = (
+                total[128:256]
+                + shift_cols(total[0:128], -rate)
+                + shift_cols(total[256:384], rate)
+            )
+            r.fga[:, px] = r.fga[:, px] + total
+
+    for h in range(ROWS):
+        r.fg[pl.ds(h, 128, stride=16), :] = r.fga[:, h * 128 : (h + 1) * 128]
+
+    for copy in sent:
+        copy.wait_send()
+
+
+def fused(features, w_one, w_atrous, w_pool, w_proj, gains, biases, out_grad):
+    zeros = jnp.zeros((16, 3), F32)
+    par = jnp.concatenate([gains.T, zeros, biases.T, jnp.zeros((16, 115), F32)], axis=1)
+    vmem = pl.BlockSpec(memory_space=pltpu.VMEM)
+    shapes = (
+        (256, 128),
+        (2048, 128),
+        (128, 256),
+        (27, 128, 256),
+        (128, 256),
+        (5, 16, 256),
+        (16, 128),
+    )
+    out, fg, dw1, dwa, dwpool, dwproj, dpar = pl.pallas_call(
+        head_kernel,
+        out_shape=[jax.ShapeDtypeStruct(s, F32) for s in shapes],
+        in_specs=[vmem] * len(INPUTS),
+        out_specs=[vmem] * len(OUTPUTS),
+        scratch_shapes=list(scratch_table(NSEMS).values()),
+        compiler_params=pltpu.CompilerParams(
+            collective_id=0, has_side_effects=True, vmem_limit_bytes=64 * 2**20
+        ),
+    )(
+        features.reshape(2048, 128),
+        out_grad.reshape(256, 128),
+        w_one,
+        w_atrous.reshape(27, 128, 256),
+        w_pool,
+        w_proj,
+        par,
+    )
+    return (
+        out.reshape(1, 16, ROWS, COLS),
+        fg.reshape(1, 128, ROWS, COLS),
+        dw1,
+        dwa.reshape(3, 9, 128, 256),
+        dwpool,
+        dwproj,
+        dpar[:, 0:5].T,
+        dpar[:, 8:13].T,
+    )
+
+
 def solution(mesh):
     placed = (
         P("dp", "chan", None, None),
@@ -192,8 +986,9 @@
         P(None, "chan"),
         P("dp", "chan", None, None),
     )
+    small = mesh.shape["dp"] == 2 and mesh.shape["chan"] == 16
     return jax.shard_map(
-        local,
+        fused if small else local,
         mesh=mesh,
         in_specs=placed,
         out_specs=(

time: 461 us -> 154 us (0.33)
  waiting for transfers between devices: 263 us -> 0 us
  Pallas kernels: 0 us -> 138 us
  blocking collectives: 59.4 us -> 0 us
  matrix products: 47.7 us -> 0 us
  local copies, waits for them, and re-layouts: 51.1 us -> 14.8 us
  other arithmetic: 23 us -> 0.68 us
  between operations: 15.1 us -> 0.66 us
    reduce_scatter x2 -> x0, waiting for transfers between devices: 168 us -> none  [the longest x1 107 us: local(): lax.psum_scatter(spatial_term, 'chan', scatter_dimension=1, tiled=True)]
    pallas_call x0 -> x1, Pallas kernels: none -> 138 us  [fused(): pl.pallas_call(head_kernel, out_shape=[jax.ShapeDtypeStruct(s, F32) for s...]
    dot_general x13 -> x0, matrix products: 47.7 us -> none  [the longest x1 13.2 us: local(): jnp.einsum('rtco,ronhw->rtnchw', w_atrous, spatial_portion[1:], preferred...]
    all_gather x2 -> x0, waiting for transfers between devices: 37.9 us -> none  [the longest x1 37 us: local(): portion = lax.all_gather(proj_low, 'chan', axis=0, tiled=True)]
    another operation x1 -> x0, blocking collectives: 31.2 us -> none
    unnamed x7 -> x0, waiting for transfers between devices: 28.7 us -> none
    psum x5 -> x0, blocking collectives: 28.2 us -> none  [the longest x1 8.36 us: local(): lax.psum(proj_wgrad.astype(jnp.bfloat16), 'dp').astype(jnp.float32)]
    psum x1 -> x0, waiting for transfers between devices: 27.8 us -> none  [local(): lax.psum(one_grad.astype(jnp.bfloat16), 'dp').astype(jnp.float32)]
  transfers between devices with their start and end apart: 6 -> 0, of which waited for: 6 -> 0; matrix products, arithmetic and copies ran while one was open for 14% -> 0% of each run, Pallas kernels for 0% -> 0%
where the time goes in v1:
time: 154 us
  Pallas kernels  138 us (90%)
  local copies, waits for them, and re-layouts  14.8 us (10%)
    pallas_call x1, Pallas kernels, fused(): pl.pallas_call(head_kernel, out_shape=[jax.ShapeDtypeStruct(s, F32) for s...  138 us
    unnamed x14, local copies, waits for them, and re-layouts  13.8 us

profile of v1, /device:TPU:0, one launch (start us, length us, event | category | flops | bytes accessed | tf_op | source)
XLA Modules:
  0.0 154.1 jit_solution(4403928875432296410)
XLA Ops:
  0.6 0.1 pad.3.clone
  0.7 0.1 pad.1.clone
  0.8 0.8 copy.16
  1.6 0.8 copy.17
  2.3 0.7 maximum_maximum_fusion.refs_6_
  3.0 138.0 %shard_map.143 = (f32[256,128]{1,0:T(8,128)}, f32[2048,128]{1,0:T(8,128)}, f32[128,256]{1,0:T(8,128)}, f32[27,128,256]{2,1,0:T(8,128)}, f32[128,256]{1,0:T(8,128...) custom-call(bf16[2048,128]{1,0:T(8,128)(2,1)} %bitcast.15, bf16[256,128]{1,0:T(8,128)(2,1)} %bitcast.17, ...), custom_call_target="tpu_custom_call" | custom-call | tf_op jit(solution)/shard_map/pallas_call | solution.py:948
  141.0 0.8 slice_bitcast_fusion
  141.9 0.7 copy.19
  142.5 0.7 copy.18
  143.2 1.6 %copy.26 = f32[1,16,16,128]{3,2,1,0:T(8,128)} copy(f32[1,16,16,128]{3,2,1,0:T(8,128)} %bitcast.16) | data formatting | bytes 262144
  144.8 2.3 %copy.27 = f32[1,128,16,128]{3,2,1,0:T(8,128)} copy(f32[1,128,16,128]{3,2,1,0:T(8,128)} %bitcast.14) | data formatting | bytes 2097152
  147.0 1.6 %copy.28 = f32[128,256]{1,0:T(8,128)} copy(f32[128,256]{1,0:T(8,128)} %get-tuple-element.42) | data formatting | bytes 262144
  148.6 0.0 copy-start
  148.6 0.0 copy-start.1
  148.6 4.2 %copy.29 = f32[3,9,128,256]{3,2,1,0:T(8,128)} copy(f32[3,9,128,256]{3,2,1,0:T(8,128)} %bitcast.12) | data formatting | bytes 7077888
  152.8 0.0 copy-done
  152.8 0.7 copy.30
  153.5 0.0 copy-done.1
  153.5 0.6 copy.31
  (2 shorter events, 0.0 us)
Async XLA Ops:
  148.6 4.2 %copy-start = (f32[128,256]{1,0:T(8,128)S(1)}, f32[128,256]{1,0:T(8,128)}, u32[]{:S(2)}) copy-start(f32[128,256]{1,0:T(8,128)} %get-tuple-element.44) | copy-start | bytes 393220
  148.6 4.9 %copy-start.1 = (f32[5,16,256]{2,1,0:T(8,128)S(1)}, f32[5,16,256]{2,1,0:T(8,128)}, u32[]{:S(2)}) copy-start(f32[5,16,256]{2,1,0:T(8,128)} %get-tuple-element.45) | copy-start | bytes 245764

commit v2 on v1

--- a/solution.py
+++ b/solution.py
@@ -225,8 +225,17 @@
 SLOTS, SPANS, NSLOTS = weight_slots()
 
 
-def width_of(branch):
-    return WIDE if branch == 0 else PIXELS
+HALVES = 2
+SPAN = PIXELS // HALVES
+PIECES = [(b, half * SPAN) for b in ORDER for half in range(HALVES)]
+
+
+def carries_pool(piece):
+    return piece == (0, PIXELS - SPAN)
+
+
+def lanes_of(piece):
+    return pl.ds(piece[1], SPAN + (128 if carries_pool(piece) else 0))
 
 
 def dot(a, b):
@@ -282,13 +291,21 @@
     return 0.5 * jnp.tanh(0.5 * z) + 0.5
 
 
-INPUTS = ("feat", "og", "w1", "wa", "wpool", "wproj", "par")
-OUTPUTS = ("out", "fg", "dw1", "dwa", "dwpool", "dwproj", "dpar")
+INPUTS = ("feat", "og", "w1", "wa", "wpool", "wproj", "gains", "biases")
+OUTPUTS = ("out", "dwpool", "dwproj", "dgains", "dbiases", "fgb", "dwb")
 
 
 def scratch_table(sems):
     vm = pltpu.VMEM
     return {
+        "feat": vm((2048, 128), BF16),
+        "og": vm((256, 128), BF16),
+        "w1": vm((128, 256), BF16),
+        "wa": vm((27, 128, 256), BF16),
+        "wpool": vm((128, 256), BF16),
+        "wproj": vm((5, 16, 256), BF16),
+        "gains": vm((5, 16), F32),
+        "biases": vm((5, 16), F32),
         "fsib": vm((2048, 128), BF16),
         "foth": vm((2048, 128), BF16),
         "x": vm((256, PIXELS), BF16),
@@ -305,7 +322,11 @@
         "pt": vm((GROUPS, 16, 128), F32),
         "wp": vm((GROUPS, 5, 16, 256), BF16),
         "wpt": vm((256, 640), BF16),
-        "xs": vm((2, 3, 3, 128, PIXELS), BF16),
+        "xv": vm((2, 7, 128, PIXELS), BF16),
+        "sl": vm((2, 4, GROUPS, 16, PIXELS), BF16),
+        "flip": vm((128, 128), F32),
+        "c1": vm((5, 128, 128), F32),
+        "c2": vm((5, 128, 128), F32),
         "act": vm((2, 4, GROUPS, 16, PIXELS), BF16),
         "ao": vm((2, 4, 16, PIXELS), BF16),
         "pa": vm((5, 128, 128), F32),
@@ -319,11 +340,15 @@
         "dp": vm((2, GROUPS, 2, 16, PIXELS), BF16),
         "dpo": vm((GROUPS, 2, 16, 128), BF16),
         "d": vm((4, 2, GROUPS, 2, 16, PIXELS), BF16),
+        "dwv": vm((28, 128, 256), BF16),
         "fga": vm((128, PIXELS), F32),
+        "fgv": vm((128, PIXELS), BF16),
         "pooled": vm((2, 128, 128), F32),
         "ppool": vm((2, 128, 128), F32),
         "ss": pltpu.SemaphoreType.DMA((sems,)),
         "rs": pltpu.SemaphoreType.DMA((sems,)),
+        "ls": pltpu.SemaphoreType.DMA((32,)),
+        "li": pltpu.SemaphoreType.DMA((8,)),
     }
 
 
@@ -331,11 +356,11 @@
     pass
 
 
-NSEMS = 160
+NSEMS = 224
 
 
 def head_kernel(*refs):
-    names = INPUTS + OUTPUTS + tuple(scratch_table(NSEMS))
+    names = tuple(n + "_hbm" for n in INPUTS) + OUTPUTS + tuple(scratch_table(NSEMS))
     r = Refs()
     for name, ref in zip(names, refs, strict=True):
         setattr(r, name, ref)
@@ -357,6 +382,7 @@
 
     counter = [0]
     sent = []
+    due = {}
 
     def new(n=1):
         first = counter[0]
@@ -378,18 +404,21 @@
         copy = rcopy(src, dst, n, device)
         copy.start()
         (sent if group is None else group).append(copy)
+        due[n] = (dst, device)
 
     def arrived(ref, n, device):
+        del due[n]
         rcopy(ref, ref, n, device).wait_recv()
 
     barrier = pltpu.get_barrier_semaphore()
     partners = [sibling, xdev, ydev] + zdev[1:]
     for partner in partners:
         pl.semaphore_signal(barrier, inc=1, device_id=partner, device_id_type=MESH)
-    pl.semaphore_wait(barrier, len(partners))
-
-    n_feat = new()
-    send(r.feat, r.fsib, n_feat, sibling)
+
+    loads = {}
+    for n, name in enumerate(("feat", "w1", "wpool", "og", "gains", "biases", "wproj", "wa")):
+        loads[name] = pltpu.make_async_copy(getattr(r, name + "_hbm"), getattr(r, name), r.li.at[n])
+        loads[name].start()
 
     rr = iota((256, 256), 0)
     cc = iota((256, 256), 1)
@@ -444,15 +473,22 @@
     g_par = Gather(lambda g: r.pt.at[g], own_group, False)
     g_wp = Gather(lambda g: r.wp.at[g], own_group, False)
     g_pre = {}
-    for b in ORDER:
-        w = width_of(b)
-        g_pre[b] = Gather(lambda g, b=b, w=w: r.g.at[b, x, g, :, pl.ds(0, w)], pre_group, True)
+    for piece in PIECES:
+        g_pre[piece] = Gather(
+            lambda g, b=piece[0], w=lanes_of(piece): r.g.at[b, x, g, :, w], pre_group, True
+        )
 
     mine = own_group(y, z)
+    loads["og"].wait()
     og = permuted(r.og, 0)
     for h in range(ROWS):
         r.ogs[x, mine, :, h * 128 : (h + 1) * 128] = og[h * 16 : (h + 1) * 16]
-    r.pt[mine] = r.par[...]
+    r.flip[...] = jnp.zeros((128, 128), F32)
+    for name in ("gains", "biases", "wproj"):
+        loads[name].wait()
+    r.flip[0:5, 0:16] = r.gains[...]
+    r.flip[8:13, 0:16] = r.biases[...]
+    r.pt[mine] = r.flip[...].T[0:16, :]
     r.wp[mine] = r.wproj[...]
 
     n_w = {b: new() for b in ORDER}
@@ -474,6 +510,8 @@
             else:
                 for j in range(3):
                     transpose_into(slot + j, weight_ref(b, i, j))
+
+    def send_weights(b):
         lo, hi = SPANS[b]
         send(
             r.tw.at[pl.ds(lo, hi - lo), :, 1 - k],
@@ -486,8 +524,6 @@
         lo, hi = SPANS[b]
         arrived(r.lw.at[pl.ds(lo, hi - lo), :, :, pl.ds(128, 128)], n_w[b], sibling)
 
-    prepare_weights(0)
-
     def place(ref, base):
         for block in range(8):
             t = permuted(ref, block)
@@ -496,12 +532,27 @@
                     h * 16 : (h + 1) * 16
                 ]
 
+    for name in ("w1", "wpool", "feat"):
+        loads[name].wait()
+    prepare_weights(0)
     place(r.feat, 0)
+    loads["wa"].wait()
+    prepare_weights(ORDER[1])
+
+    pl.semaphore_wait(barrier, len(partners))
+
+    n_feat = new()
+    n_foth = new()
+    send(r.feat, r.fsib, n_feat, sibling)
+    send_weights(0)
+    send_weights(ORDER[1])
+    send(r.feat, r.foth, n_foth, xdev)
     arrived(r.fsib, n_feat, sibling)
     place(r.fsib, 128)
 
-    def convolve(b):
-        for q in range(PIXELS // BLOCK):
+    def convolve(piece):
+        b = piece[0]
+        for q in range(piece[1] // BLOCK, (piece[1] + SPAN) // BLOCK):
             px = slice(q * BLOCK, (q + 1) * BLOCK)
             total = None
             for i, offset in branch_rows(b):
@@ -521,7 +572,7 @@
                     + shift_cols(total[256:384], -rate)
                 )
             r.acc[b, :, :, px] = total.reshape(GROUPS, 16, BLOCK)
-        if b == 0:
+        if carries_pool(piece):
             pooled = jnp.zeros((256, 128), F32)
             for h in range(ROWS):
                 pooled = pooled + r.x[:, h * 128 : (h + 1) * 128].astype(F32)
@@ -532,58 +583,55 @@
             sums = lane_sum(dot(r.lw[slot].reshape(128, 256), terms))
             r.acp[...] = jnp.broadcast_to(sums, (128, 128)).reshape(GROUPS, 16, 128)
 
-    n_ry = {b: new() for b in ORDER}
-    n_rz = {b: new(3) for b in ORDER}
-
-    def reduce_y_send(b):
-        w = width_of(b)
-        r.ys[b, :, :, 0:PIXELS] = r.acc[b, pl.ds(4 * (1 - y), 4)].astype(BF16)
-        if b == 0:
+    n_ry = {piece: new() for piece in PIECES}
+    n_rz = {piece: new(3) for piece in PIECES}
+
+    def reduce_y_send(piece):
+        b, w = piece[0], lanes_of(piece)
+        px = pl.ds(piece[1], SPAN)
+        r.ys[b, :, :, px] = r.acc[b, pl.ds(4 * (1 - y), 4), :, px].astype(BF16)
+        if carries_pool(piece):
             r.ys[b, :, :, PIXELS:WIDE] = encode_pair(r.acp[pl.ds(4 * (1 - y), 4)])
-        send(r.ys.at[b, :, :, pl.ds(0, w)], r.yr.at[b, :, :, pl.ds(0, w)], n_ry[b], ydev)
-
-    def reduce_z_send(b):
-        w = width_of(b)
-        arrived(r.yr.at[b, :, :, pl.ds(0, w)], n_ry[b], ydev)
-        for i in (1, 2, 3, 0):
+        send(r.ys.at[b, :, :, w], r.yr.at[b, :, :, w], n_ry[piece], ydev)
+
+    def reduce_z_send(piece):
+        b, w = piece[0], lanes_of(piece)
+        px = pl.ds(piece[1], SPAN)
+        arrived(r.yr.at[b, :, :, w], n_ry[piece], ydev)
+        for i in (2, 1, 3, 0):
             zz = z if i == 0 else zpos[i]
             g = 4 * y + zz
-            s = r.acc[b, g] + r.yr[b, zz, :, 0:PIXELS].astype(F32)
-            if b == 0:
+            s = r.acc[b, g, :, px] + r.yr[b, zz, :, px].astype(F32)
+            if carries_pool(piece):
                 e = r.acp[g] + decode_pair(r.yr[b, zz, :, PIXELS:WIDE])
             if i == 0:
-                r.acc[b, g] = s
-                if b == 0:
+                r.acc[b, g, :, px] = s
+                if carries_pool(piece):
                     r.acp[g] = e
             else:
-                r.zs[b, i, :, 0:PIXELS] = s.astype(BF16)
-                if b == 0:
+                r.zs[b, i, :, px] = s.astype(BF16)
+                if carries_pool(piece):
                     r.zs[b, i, :, PIXELS:WIDE] = encode_pair(e)
-                send(
-                    r.zs.at[b, i, :, pl.ds(0, w)],
-                    r.zr.at[b, i, :, pl.ds(0, w)],
-                    n_rz[b] + i - 1,
-                    zdev[i],
-                )
-
-    def reduce_finish(b):
-        w = width_of(b)
+                send(r.zs.at[b, i, :, w], r.zr.at[b, i, :, w], n_rz[piece] + i - 1, zdev[i])
+
+    def reduce_finish(piece):
+        b, w = piece[0], lanes_of(piece)
+        px = pl.ds(piece[1], SPAN)
         g = pre_group(y, z)
-        total = r.acc[b, g]
-        extra = r.acp[g] if b == 0 else None
+        total = r.acc[b, g, :, px]
+        extra = r.acp[g] if carries_pool(piece) else None
         for i in (1, 2, 3):
-            arrived(r.zr.at[b, i, :, pl.ds(0, w)], n_rz[b] + i - 1, zdev[i])
-            total = total + r.zr[b, i, :, 0:PIXELS].astype(F32)
-            if b == 0:
+            arrived(r.zr.at[b, i, :, w], n_rz[piece] + i - 1, zdev[i])
+            total = total + r.zr[b, i, :, px].astype(F32)
+            if carries_pool(piece):
                 extra = extra + decode_pair(r.zr[b, i, :, PIXELS:WIDE])
-        r.g[b, x, g, :, 0:PIXELS] = total.astype(BF16)
-        if b == 0:
+        r.g[b, x, g, :, px] = total.astype(BF16)
+        if carries_pool(piece):
             r.g[b, x, g, :, PIXELS:WIDE] = encode_pair(extra)
-        g_pre[b].start()
-
-    def other_pre(b):
-        w = width_of(b)
-        return lambda g: r.g.at[b, 1 - x, g, :, pl.ds(0, w)]
+        g_pre[piece].start()
+
+    def other_pre(piece):
+        return lambda g: r.g.at[piece[0], 1 - x, g, :, lanes_of(piece)]
 
     shift_pairs = []
     lane_r = iota((128, 128), 0)
@@ -592,6 +640,13 @@
         left = jnp.where(lane_r == lane_c - rate, 1.0, 0.0).astype(BF16)
         right = jnp.where(lane_r == lane_c + rate, 1.0, 0.0).astype(BF16)
         shift_pairs.append(jnp.concatenate([left, right], axis=1))
+
+    local = []
+
+    def keep(src, dst):
+        copy = pltpu.make_async_copy(src, dst, r.ls.at[len(local)])
+        copy.start()
+        local.append(copy)
 
     def place_shifted(ref, image):
         for block in range(8):
@@ -602,85 +657,119 @@
                 for h in range(ROWS):
                     px = slice(h * 128, (h + 1) * 128)
                     hc = slice(h * 16, (h + 1) * 16)
-                    r.xs[image, a, 0, rows, px] = both[hc, 0:128]
-                    r.xs[image, a, 1, rows, px] = t[hc]
-                    r.xs[image, a, 2, rows, px] = both[hc, 128:256]
-
-    n_foth = new()
+                    if a == 0:
+                        r.xv[image, 0, rows, px] = t[hc]
+                    r.xv[image, 1 + 2 * a, rows, px] = both[hc, 0:128]
+                    r.xv[image, 2 + 2 * a, rows, px] = both[hc, 128:256]
 
     count = float(2 * PIXELS)
 
-    def finish_norm(b, rows, s, q, gain, bias):
-        mean = lane_sum(s) / count
-        inv = lax.rsqrt(lane_sum(q) / count - mean * mean + norm_eps)
-        scale = gain * inv
-        r.pa[b, rows] = jnp.broadcast_to(scale, (16, 128))
-        r.pb[b, rows] = jnp.broadcast_to(bias - mean * scale, (16, 128))
-        r.pm[b, rows] = jnp.broadcast_to(mean, (16, 128))
-        r.pi[b, rows] = jnp.broadcast_to(inv, (16, 128))
+    def each_group(body):
+        def step(g, _):
+            body(g, pl.ds(pl.multiple_of(g * 16, 16), 16))
+            return 0
+
+        lax.fori_loop(0, GROUPS, step, 0)
+
+    tiles = [(image, slice(h * 128, (h + 1) * 128)) for image in range(2) for h in range(ROWS)]
+    zero_tile = jnp.zeros((16, 128), F32)
+
+    def spread_lanes(column):
+        return jnp.broadcast_to(column, (128, 128))
+
+    def norm_params(b):
+        mean = lane_sum(r.s1[b]) / count
+        inv = lax.rsqrt(lane_sum(r.s2[b]) / count - mean * mean + norm_eps)
+        par = r.pt[...].reshape(128, 128)
+        scale = par[:, b : b + 1] * inv
+        r.pa[b] = spread_lanes(scale)
+        r.pb[b] = spread_lanes(par[:, 8 + b : 9 + b] - mean * scale)
+        r.pm[b] = spread_lanes(mean)
+        r.pi[b] = spread_lanes(inv)
+
+    def grad_params(b):
+        s1 = lane_sum(r.s1[b])
+        inv, mean = r.pi[b][:, 0:1], r.pm[b][:, 0:1]
+        s2 = (lane_sum(r.s2[b]) - mean * s1) * inv
+        scale = r.pa[b][:, 0:1]
+        c2 = -scale * inv * s2 / count
+        r.s1[b] = spread_lanes(s1)
+        r.s2[b] = spread_lanes(s2)
+        r.c2[b] = spread_lanes(c2)
+        r.c1[b] = spread_lanes(-scale * s1 / count - mean * c2)
+
+    def act_and_slope(zed):
+        u = 0.5 * jnp.tanh(0.5 * zed)
+        sg = 0.5 + u
+        act = zed * sg
+        return act, sg + act * (0.5 - u)
 
     def branch_norm(b):
-        def group(g, _):
-            rows = pl.ds(pl.multiple_of(g * 16, 16), 16)
-            s = jnp.zeros((16, 128), F32)
-            q = jnp.zeros((16, 128), F32)
-            for image in range(2):
-                for h in range(ROWS):
-                    v = r.g[b, image, g, :, h * 128 : (h + 1) * 128].astype(F32)
-                    s = s + v
-                    q = q + v * v
-            par = r.pt[g]
-            finish_norm(b, rows, s, q, par[:, b : b + 1], par[:, 8 + b : 9 + b])
+        def sums(g, rows):
+            s, q = zero_tile, zero_tile
+            for image, px in tiles:
+                v = r.g[b, image, g, :, px].astype(F32)
+                s = s + v
+                q = q + v * v
+            r.s1[b, rows] = s
+            r.s2[b, rows] = q
+
+        each_group(sums)
+        norm_params(b)
+
+        def apply(g, rows):
             scale, base = r.pa[b, rows], r.pb[b, rows]
-            for image in range(2):
-                for h in range(ROWS):
-                    px = slice(h * 128, (h + 1) * 128)
-                    zed = r.g[b, image, g, :, px].astype(F32) * scale + base
-                    r.act[image, b, g, :, px] = (zed * sigmoid(zed)).astype(BF16)
-            return 0
-
-        lax.fori_loop(0, GROUPS, group, 0)
+            for image, px in tiles:
+                act, slope = act_and_slope(r.g[b, image, g, :, px].astype(F32) * scale + base)
+                r.act[image, b, g, :, px] = act.astype(BF16)
+                r.sl[image, b, g, :, px] = slope.astype(BF16)
+
+        each_group(apply)
 
     g_par.start()
     g_wp.start()
-    steps = len(ORDER)
-    for s in range(steps + 3):
+    steps = len(PIECES)
+    for s in range(steps + 4):
         if s < steps:
-            b = ORDER[s]
-            wait_weights(b)
-            convolve(b)
-            reduce_y_send(b)
-            if s + 1 < steps:
-                prepare_weights(ORDER[s + 1])
-        if s == 0:
+            b = PIECES[s][0]
+            if s % HALVES == 0:
+                wait_weights(b)
+            convolve(PIECES[s])
+            reduce_y_send(PIECES[s])
+            if s % HALVES == 0 and s // HALVES + 2 < len(ORDER):
+                prepare_weights(ORDER[s // HALVES + 2])
+                send_weights(ORDER[s // HALVES + 2])
+        if 1 <= s <= steps:
+            reduce_z_send(PIECES[s - 1])
+        if s == 1:
             g_og.start()
-        if 1 <= s <= steps:
-            reduce_z_send(ORDER[s - 1])
-        if s == 1:
+        if s == 2:
             g_par.forward_z()
             g_wp.forward_z()
             g_og.forward_z()
-        if s == 2:
+        if 2 <= s <= steps + 1:
+            reduce_finish(PIECES[s - 2])
+        if s == 4:
             g_par.forward_y()
             g_wp.forward_y()
-        if 2 <= s <= steps + 1:
-            reduce_finish(ORDER[s - 2])
-        if s == 3:
+        if 3 <= s <= steps + 2:
+            g_pre[PIECES[s - 3]].forward_z()
+        if s >= 4:
+            g_pre[PIECES[s - 4]].forward_y()
+        if s == steps - 2:
             place_shifted(r.feat, x)
-        if 3 <= s <= steps + 2:
-            g_pre[ORDER[s - 3]].forward_z()
-        if s >= 4:
-            g_pre[ORDER[s - 4]].forward_y()
-    g_pre[ORDER[steps - 1]].forward_y()
+        if s == steps - 1:
+            arrived(r.foth, n_foth, xdev)
+            place_shifted(r.foth, 1 - x)
     g_og.forward_y()
-    send(r.feat, r.foth, n_foth, xdev)
 
     for b in range(5):
         r.wpt[:, b * 128 : (b + 1) * 128] = dot_nt(eye, r.wp[:, b].reshape(128, 256)).astype(BF16)
 
-    for b in ORDER:
-        g_pre[b].finish(other_pre(b))
-        branch_norm(b)
+    for piece in PIECES:
+        g_pre[piece].finish(other_pre(piece))
+        if piece[1] == PIXELS - SPAN:
+            branch_norm(piece[0])
 
     pool_act = []
     lane128 = iota((128, 128), 1)
@@ -712,51 +801,45 @@
     for image in range(2):
         arrived(r.pr.at[image], n_pp + image, sibling)
 
-    def proj_group(g, _):
-        rows = pl.ds(pl.multiple_of(g * 16, 16), 16)
-        s = jnp.zeros((16, 128), F32)
-        q = jnp.zeros((16, 128), F32)
-        for image in range(2):
+    def proj_sums(g, rows):
+        s, q = zero_tile, zero_tile
+        for image, px in tiles:
+            v = r.acc[2 * image + k, g, :, px] + r.pr[image, g, :, px]
+            r.pr[image, g, :, px] = v
+            s = s + v
+            q = q + v * v
+        r.s1[4, rows] = s
+        r.s2[4, rows] = q
+
+    each_group(proj_sums)
+    norm_params(4)
+
+    def proj_slope(g, rows):
+        scale, base = r.pa[4, rows], r.pb[4, rows]
+        s1, s2 = zero_tile, zero_tile
+        for image, px in tiles:
+            v = r.pr[image, g, :, px]
+            _, slope = act_and_slope(v * scale + base)
+            dz = r.ogs[image, g, :, px].astype(F32) * slope
+            r.dzp[image, g, :, px] = dz
+            s1 = s1 + dz
+            s2 = s2 + dz * v
+        r.s1[4, rows] = s1
+        r.s2[4, rows] = s2
+
+    each_group(proj_slope)
+    grad_params(4)
+    n_dp = new(2)
+    for image in range(2):
+
+        def proj_low(g, rows, image=image):
+            scale, c1, c2 = r.pa[4, rows], r.c1[4, rows], r.c2[4, rows]
             for h in range(ROWS):
                 px = slice(h * 128, (h + 1) * 128)
-                v = r.acc[2 * image + k, g, :, px] + r.pr[image, g, :, px]
-                r.pr[image, g, :, px] = v
-                s = s + v
-                q = q + v * v
-        par = r.pt[g]
-        finish_norm(4, rows, s, q, par[:, 4:5], par[:, 12:13])
-        scale, base = r.pa[4, rows], r.pb[4, rows]
-        mean, inv = r.pm[4, rows], r.pi[4, rows]
-        s1 = jnp.zeros((16, 128), F32)
-        s2 = jnp.zeros((16, 128), F32)
-        for image in range(2):
-            for h in range(ROWS):
-                px = slice(h * 128, (h + 1) * 128)
-                v = r.pr[image, g, :, px]
-                zed = v * scale + base
-                sg = sigmoid(zed)
-                dz = r.ogs[image, g, :, px].astype(F32) * (sg * (1.0 + zed * (1.0 - sg)))
-                r.dzp[image, g, :, px] = dz
-                s1 = s1 + dz
-                s2 = s2 + dz * (v - mean)
-        s1 = jnp.broadcast_to(lane_sum(s1), (16, 128))
-        s2 = jnp.broadcast_to(lane_sum(s2), (16, 128)) * inv
-        r.s1[4, rows] = s1
-        r.s2[4, rows] = s2
-        c1 = -scale * s1 / count
-        c2 = -scale * inv * s2 / count
-        for image in range(2):
-            for h in range(ROWS):
-                px = slice(h * 128, (h + 1) * 128)
-                v = r.pr[image, g, :, px]
-                low = scale * r.dzp[image, g, :, px] + ((v - mean) * c2 + c1)
+                low = scale * r.dzp[image, g, :, px] + (r.pr[image, g, :, px] * c2 + c1)
                 r.dp[image, g, k, :, px] = low.astype(BF16)
-        return 0
-
-    lax.fori_loop(0, GROUPS, proj_group, 0)
-
-    n_dp = new(2)
-    for image in range(2):
+
+        each_group(proj_low)
         ref = r.dp.at[image, :, k]
         send(ref, ref, n_dp + image, sibling)
 
@@ -768,6 +851,99 @@
 
     for image in range(2):
         arrived(r.dp.at[image, :, 1 - k], n_dp + image, sibling)
+
+    for copy in pp_sent:
+        copy.wait_send()
+    n_d = {b: new(2) for b in ORDER}
+
+    def branch_back(b, turn):
+        weights = r.wp[:, b].reshape(128, 256)
+        for image in range(2):
+            for q in range(PIXELS // 512):
+                px = slice(q * 512, (q + 1) * 512)
+                back = dot(weights, r.dp[image, :, :, :, px].reshape(256, 512))
+                r.acc[2 * turn + image, :, :, px] = back.reshape(GROUPS, 16, 512)
+
+        def slope(g, rows):
+            s1, s2 = zero_tile, zero_tile
+            for image, px in tiles:
+                dz = r.acc[2 * turn + image, g, :, px] * r.sl[image, b, g, :, px].astype(F32)
+                r.acc[2 * turn + image, g, :, px] = dz
+                s1 = s1 + dz
+                s2 = s2 + dz * r.g[b, image, g, :, px].astype(F32)
+            r.s1[b, rows] = s1
+            r.s2[b, rows] = s2
+
+        each_group(slope)
+        grad_params(b)
+        for image in range(2):
+
+            def lower(g, rows, image=image):
+                scale, c1, c2 = r.pa[b, rows], r.c1[b, rows], r.c2[b, rows]
+                for h in range(ROWS):
+                    px = slice(h * 128, (h + 1) * 128)
+                    v = r.g[b, image, g, :, px].astype(F32)
+                    low = scale * r.acc[2 * turn + image, g, :, px] + (v * c2 + c1)
+                    r.d[b, image, g, k, :, px] = low.astype(BF16)
+
+            each_group(lower)
+            there = r.d.at[b, image, :, k]
+            send(there, there, n_d[b] + image, sibling)
+
+    def branch_grads(b, first_branch, last_branch):
+        for image in range(2):
+            arrived(r.d.at[b, image, :, 1 - k], n_d[b] + image, sibling)
+        planes = (2 * b - 1, 0, 2 * b)
+        for i, offset in branch_rows(b):
+            first, last = max(0, -offset), min(ROWS, ROWS - offset)
+            there = slice((first + offset) * 128, (last + offset) * 128)
+            here = slice(first * 128, last * 128)
+            total = None
+            for image in range(2):
+                if b == 0:
+                    rows = r.xv[image, 0]
+                else:
+                    rows = jnp.concatenate([r.xv[image, p, :, there] for p in planes], axis=0)
+                part = dot_nt(rows, r.d[b, image, :, :, :, here].reshape(256, -1))
+                total = part if total is None else total + part
+            total = total.astype(BF16)
+            if b == 0:
+                slot = pl.ds(27, 1)
+                r.dwv[27] = total
+            else:
+                slot = pl.ds((b - 1) * 9 + 3 * i, 3)
+                r.dwv[slot] = total.reshape(3, 128, 256)
+            keep(r.dwv.at[slot], r.dwb.at[slot])
+        for q in range(PIXELS // BLOCK):
+            px = slice(q * BLOCK, (q + 1) * BLOCK)
+            total = None
+            for i, offset in branch_rows(b):
+                source = q - offset * COLS // BLOCK
+                if source < 0 or source >= PIXELS // BLOCK:
+                    continue
+                if b == 0:
+                    weights = r.w1[...]
+                else:
+                    weights = r.wa[pl.ds((b - 1) * 9 + 3 * i, 3)].reshape(384, 256)
+                dblock = r.d[b, x, :, :, :, source * BLOCK : (source + 1) * BLOCK]
+                part = dot(weights, dblock.reshape(256, BLOCK))
+                total = part if total is None else total + part
+            if b:
+                rate = atrous_rates[b - 1]
+                total = (
+                    total[128:256]
+                    + shift_cols(total[0:128], -rate)
+                    + shift_cols(total[256:384], rate)
+                )
+            if not first_branch:
+                total = total + r.fga[:, px]
+            if last_branch:
+                r.fgv[:, px] = (total + fg_pool).astype(BF16)
+            else:
+                r.fga[:, px] = total
+
+    back_order = (1, 2, 3, 0)
+    branch_back(back_order[0], 0)
 
     ones = jnp.ones((PIXELS, 128), BF16)
     wp4 = r.wp[:, 4].reshape(128, 256)
@@ -779,12 +955,12 @@
         row_sums = dot(dps, ones)[:, 0:1]
         pool_grad = lane_sum(dot(wp4, split_lanes(row_sums).astype(BF16)))
         pre = r.ppool[image][:, 0:1]
-        sg = sigmoid(pre)
-        low = (pool_grad * (sg * (1.0 + pre * (1.0 - sg)))).astype(BF16).astype(F32)
+        _, slope = act_and_slope(pre)
+        low = (pool_grad * slope).astype(BF16).astype(F32)
         for lane in (image, image + 2, image + 4):
             dpo = dpo + jnp.where(lane128 == lane, low, 0.0)
-        mine_pre = r.ppool[image, my_rows][:, 0:1]
-        mine_act = (mine_pre * sigmoid(mine_pre)).astype(BF16).astype(F32)
+        mine_act, _ = act_and_slope(r.ppool[image, my_rows][:, 0:1])
+        mine_act = mine_act.astype(BF16).astype(F32)
         dwp4 = dwp4 + mine_act * dot_nt(jnp.ones((16, PIXELS), BF16), dps)
     r.dwproj[4] = dwp4
     r.dpo[:, k] = dpo.astype(BF16).reshape(GROUPS, 16, 128)
@@ -792,81 +968,33 @@
     ref = r.dpo.at[:, k]
     send(ref, ref, n_dpo, sibling)
 
+    branch_back(back_order[1], 1)
+    branch_grads(back_order[0], True, False)
+    branch_back(back_order[2], 0)
+
     dwp = jnp.zeros((64, 256), F32)
     for image in range(2):
         dwp = dwp + dot_nt(r.ao[image].reshape(64, PIXELS), r.dp[image].reshape(256, PIXELS))
     r.dwproj[0:4] = dwp.reshape(4, 16, 256)
 
-    for copy in pp_sent:
-        copy.wait_send()
-    for image in range(2):
-        for q in range(PIXELS // BLOCK):
-            px = slice(q * BLOCK, (q + 1) * BLOCK)
-            dblock = r.dp[image, :, :, :, px].reshape(256, BLOCK)
-            for b in range(4):
-                part = dot(r.wp[:, b].reshape(128, 256), dblock)
-                r.acc[b, :, :, px] = part.reshape(GROUPS, 16, BLOCK)
-        for b in ORDER:
-
-            def slope_group(g, _, b=b, image=image):
-                rows = pl.ds(pl.multiple_of(g * 16, 16), 16)
-                scale, base, mean = r.pa[b, rows], r.pb[b, rows], r.pm[b, rows]
-                s1 = jnp.zeros((16, 128), F32)
-                s2 = jnp.zeros((16, 128), F32)
-                for h in range(ROWS):
-                    px = slice(h * 128, (h + 1) * 128)
-                    v = r.g[b, image, g, :, px].astype(F32)
-                    zed = v * scale + base
-                    sg = sigmoid(zed)
-                    dz = r.acc[b, g, :, px] * (sg * (1.0 + zed * (1.0 - sg)))
-                    s1 = s1 + dz
-                    s2 = s2 + dz * (v - mean)
-                    r.act[image, b, g, :, px] = dz.astype(BF16)
-                if image == 0:
-                    r.s1[b, rows] = s1
-                    r.s2[b, rows] = s2
-                else:
-                    r.s1[b, rows] = jnp.broadcast_to(lane_sum(r.s1[b, rows] + s1), (16, 128))
-                    r.s2[b, rows] = jnp.broadcast_to(lane_sum(r.s2[b, rows] + s2), (16, 128)) * (
-                        r.pi[b, rows]
-                    )
-                return 0
-
-            lax.fori_loop(0, GROUPS, slope_group, 0)
-
-    n_d = {b: new(2) for b in ORDER}
-    for b in ORDER:
-        for image in range(2):
-
-            def low_group(g, _, b=b, image=image):
-                rows = pl.ds(pl.multiple_of(g * 16, 16), 16)
-                scale, mean = r.pa[b, rows], r.pm[b, rows]
-                c1 = -scale * r.s1[b, rows] / count
-                c2 = -scale * r.pi[b, rows] * r.s2[b, rows] / count
-                for h in range(ROWS):
-                    px = slice(h * 128, (h + 1) * 128)
-                    v = r.g[b, image, g, :, px].astype(F32)
-                    low = scale * r.act[image, b, g, :, px].astype(F32) + ((v - mean) * c2 + c1)
-                    r.d[b, image, g, k, :, px] = low.astype(BF16)
-                return 0
-
-            lax.fori_loop(0, GROUPS, low_group, 0)
-            ref = r.d.at[b, image, :, k]
-            send(ref, ref, n_d[b] + image, sibling)
+    branch_grads(back_order[1], False, False)
+    branch_back(back_order[3], 1)
 
     tile = jnp.zeros((16, 128), F32)
     for b in range(5):
         tile = tile + jnp.where(lane16 == b, r.s2[b, my_rows], 0.0)
         tile = tile + jnp.where(lane16 == 8 + b, r.s1[b, my_rows], 0.0)
-    r.dpar[...] = tile
-
-    arrived(r.foth, n_foth, xdev)
-    place_shifted(r.foth, 1 - x)
+    r.flip[0:16, :] = tile
+    flipped = r.flip[...].T
+    r.dgains[...] = flipped[0:5, 0:16]
+    r.dbiases[...] = flipped[8:13, 0:16]
+
+    branch_grads(back_order[2], False, False)
+
     pooled = jnp.zeros((128, 128), F32)
     for h in range(ROWS):
-        pooled = pooled + r.xs[1 - x, 0, 1, :, h * 128 : (h + 1) * 128].astype(F32)
-    r.pooled[1 - x] = jnp.broadcast_to(lane_sum(pooled) / PIXELS, (128, 128))
-
+        pooled = pooled + r.xv[1 - x, 0, :, h * 128 : (h + 1) * 128].astype(F32)
+    r.pooled[1 - x] = spread_lanes(lane_sum(pooled) / PIXELS)
     arrived(r.dpo.at[:, 1 - k], n_dpo, sibling)
     dpo = r.dpo[...].reshape(256, 128)
     pooled = jnp.zeros((128, 128), F32)
@@ -876,80 +1004,94 @@
     spread = dot(r.wpool[...], dpo)
     fg_pool = lane_sum(jnp.where(lane128 == x, spread, 0.0)) / PIXELS
 
-    for b in ORDER:
-        for image in range(2):
-            arrived(r.d.at[b, image, :, 1 - k], n_d[b] + image, sibling)
-        if b == 0:
-            total = jnp.zeros((128, 256), F32)
-            for image in range(2):
-                total = total + dot_nt(r.xs[image, 0, 1], r.d[0, image].reshape(256, PIXELS))
-            r.dw1[...] = total
-        else:
-            met = dict(branch_rows(b))
-            for i in range(3):
-                where = pl.ds((b - 1) * 9 + 3 * i, 3)
-                if i not in met:
-                    r.dwa[where] = jnp.zeros((3, 128, 256), F32)
-                    continue
-                offset = met[i]
-                first, last = max(0, -offset), min(ROWS, ROWS - offset)
-                there = slice((first + offset) * 128, (last + offset) * 128)
-                here = slice(first * 128, last * 128)
-                total = jnp.zeros((384, 256), F32)
-                for image in range(2):
-                    total = total + dot_nt(
-                        r.xs[image, b - 1, :, :, there].reshape(384, (last - first) * 128),
-                        r.d[b, image, :, :, :, here].reshape(256, (last - first) * 128),
-                    )
-                r.dwa[where] = total.reshape(3, 128, 256)
-        for q in range(PIXELS // BLOCK):
-            px = slice(q * BLOCK, (q + 1) * BLOCK)
-            if b == 0:
-                part = dot(r.w1[...], r.d[0, x, :, :, :, px].reshape(256, BLOCK)) + fg_pool
-                r.fga[:, px] = part
-                continue
-            total = None
-            for i, offset in branch_rows(b):
-                source = q - offset * COLS // BLOCK
-                if source < 0 or source >= PIXELS // BLOCK:
-                    continue
-                weights = r.wa[pl.ds((b - 1) * 9 + 3 * i, 3)].reshape(384, 256)
-                dblock = r.d[b, x, :, :, :, source * BLOCK : (source + 1) * BLOCK]
-                part = dot(weights, dblock.reshape(256, BLOCK))
-                total = part if total is None else total + part
-            rate = atrous_rates[b - 1]
-            total = (
-                total[128:256]
-                + shift_cols(total[0:128], -rate)
-                + shift_cols(total[256:384], rate)
-            )
-            r.fga[:, px] = r.fga[:, px] + total
-
-    for h in range(ROWS):
-        r.fg[pl.ds(h, 128, stride=16), :] = r.fga[:, h * 128 : (h + 1) * 128]
-
+    branch_grads(back_order[3], False, True)
+    keep(r.fgv, r.fgb)
     for copy in sent:
         copy.wait_send()
+    for copy in local:
+        copy.wait()
+
+
+COPY_INPUTS = ("out", "dwpool", "dwproj", "dgains", "dbiases", "fgb", "dwb")
+COPY_OUTPUTS = ("out_o", "dwpool_o", "dwproj_o", "dgains_o", "dbiases_o", "fg", "dw1", "dwa")
+COPY_SCRATCH = {
+    "outv": pltpu.VMEM((256, 128), F32),
+    "dwpoolv": pltpu.VMEM((128, 256), F32),
+    "dwprojv": pltpu.VMEM((5, 16, 256), F32),
+    "fgbv": pltpu.VMEM((128, PIXELS), BF16),
+    "dwbv": pltpu.VMEM((28, 128, 256), BF16),
+    "fgv": pltpu.VMEM((2048, 128), F32),
+    "dwv": pltpu.VMEM((28, 128, 256), F32),
+    "si": pltpu.SemaphoreType.DMA((16,)),
+    "so": pltpu.SemaphoreType.DMA((16,)),
+}
+
+
+def copy_kernel(*refs):
+    r = Refs()
+    names = COPY_INPUTS + COPY_OUTPUTS + tuple(COPY_SCRATCH)
+    for name, ref in zip(names, refs, strict=True):
+        setattr(r, name, ref)
+    loads = []
+    stores = []
+
+    def load(src, dst):
+        copy = pltpu.make_async_copy(src, dst, r.si.at[len(loads)])
+        copy.start()
+        loads.append(copy)
+        return copy
+
+    def store(src, dst):
+        copy = pltpu.make_async_copy(src, dst, r.so.at[len(stores)])
+        copy.start()
+        stores.append(copy)
+
+    met = [
+        (b - 1) * 9 + 3 * i for b in (1, 2, 3) for i in range(3) if i in dict(branch_rows(b))
+    ]
+    taps = [(n, load(r.dwb.at[pl.ds(n, 3)], r.dwbv.at[pl.ds(n, 3)])) for n in met]
+    one = load(r.dwb.at[pl.ds(27, 1)], r.dwbv.at[pl.ds(27, 1)])
+    fg = load(r.fgb, r.fgbv)
+    passed = [
+        (load(getattr(r, name), getattr(r, name + "v")), name)
+        for name in ("out", "dwpool", "dwproj")
+    ]
+    r.dgains_o[...] = r.dgains[...]
+    r.dbiases_o[...] = r.dbiases[...]
+    for n in range(0, 27, 3):
+        if n not in met:
+            r.dwv[n : n + 3] = jnp.zeros((3, 128, 256), F32)
+            store(r.dwv.at[pl.ds(n, 3)], r.dwa.at[pl.ds(n, 3)])
+    for n, copy in taps:
+        copy.wait()
+        r.dwv[n : n + 3] = r.dwbv[n : n + 3].astype(F32)
+        store(r.dwv.at[pl.ds(n, 3)], r.dwa.at[pl.ds(n, 3)])
+    one.wait()
+    r.dwv[27] = r.dwbv[27].astype(F32)
+    store(r.dwv.at[27], r.dw1)
+    fg.wait()
+    for h in range(ROWS):
+        r.fgv[pl.ds(h, 128, stride=16), :] = r.fgbv[:, h * 128 : (h + 1) * 128].astype(F32)
+    store(r.fgv, r.fg)
+    for copy, name in passed:
+        copy.wait()
+        store(getattr(r, name + "v"), getattr(r, name + "_o"))
+    for copy in stores:
+        copy.wait()
 
 
 def fused(features, w_one, w_atrous, w_pool, w_proj, gains, biases, out_grad):
-    zeros = jnp.zeros((16, 3), F32)
-    par = jnp.concatenate([gains.T, zeros, biases.T, jnp.zeros((16, 115), F32)], axis=1)
     vmem = pl.BlockSpec(memory_space=pltpu.VMEM)
-    shapes = (
-        (256, 128),
-        (2048, 128),
-        (128, 256),
-        (27, 128, 256),
-        (128, 256),
-        (5, 16, 256),
-        (16, 128),
-    )
-    out, fg, dw1, dwa, dwpool, dwproj, dpar = pl.pallas_call(
+    hbm = pl.BlockSpec(memory_space=pl.ANY)
+    passed = [(256, 128), (128, 256), (5, 16, 256), (5, 16), (5, 16)]
+    shapes = [jax.ShapeDtypeStruct(s, F32) for s in passed]
+    shapes.append(jax.ShapeDtypeStruct((128, PIXELS), BF16))
+    shapes.append(jax.ShapeDtypeStruct((28, 128, 256), BF16))
+    parts = pl.pallas_call(
         head_kernel,
-        out_shape=[jax.ShapeDtypeStruct(s, F32) for s in shapes],
-        in_specs=[vmem] * len(INPUTS),
-        out_specs=[vmem] * len(OUTPUTS),
+        out_shape=shapes,
+        in_specs=[hbm] * len(INPUTS),
+        out_specs=[vmem] * 5 + [hbm] * 2,
         scratch_shapes=list(scratch_table(NSEMS).values()),
         compiler_params=pltpu.CompilerParams(
             collective_id=0, has_side_effects=True, vmem_limit_bytes=64 * 2**20
@@ -961,8 +1103,18 @@
         w_atrous.reshape(27, 128, 256),
         w_pool,
         w_proj,
-        par,
-    )
+        gains,
+        biases,
+    )
+    result = passed + [(2048, 128), (128, 256), (27, 128, 256)]
+    out, dwpool, dwproj, dgains, dbiases, fg, dw1, dwa = pl.pallas_call(
+        copy_kernel,
+        out_shape=[jax.ShapeDtypeStruct(s, F32) for s in result],
+        in_specs=[hbm] * 3 + [vmem] * 2 + [hbm] * 2,
+        out_specs=[hbm] * 3 + [vmem] * 2 + [hbm] * 3,
+        scratch_shapes=list(COPY_SCRATCH.values()),
+        compiler_params=pltpu.CompilerParams(vmem_limit_bytes=64 * 2**20),
+    )(*parts)
     return (
         out.reshape(1, 16, ROWS, COLS),
         fg.reshape(1, 128, ROWS, COLS),
@@ -970,8 +1122,8 @@
         dwa.reshape(3, 9, 128, 256),
         dwpool,
         dwproj,
-        dpar[:, 0:5].T,
-        dpar[:, 8:13].T,
+        dgains,
+        dbiases,
     )
 
 

time: 154 us -> 122 us (0.79)
  Pallas kernels: 138 us -> 121 us
  local copies, waits for them, and re-layouts: 14.8 us -> 0 us
    pallas_call x1 -> x2, Pallas kernels: 138 us -> 121 us  [the longest x1 116 us: fused(): pl.pallas_call(head_kernel, out_shape=shapes, in_specs=[hbm] * len(INPUTS...]
    unnamed x14 -> x0, local copies, waits for them, and re-layouts: 13.8 us -> none
where the time goes in v2:
time: 122 us
  Pallas kernels  121 us (99%)
    pallas_call x1, Pallas kernels, fused(): pl.pallas_call(head_kernel, out_shape=shapes, in_specs=[hbm] * len(INPUTS...  116 us
    pallas_call x1, Pallas kernels, fused(): pl.pallas_call(copy_kernel, out_shape=[jax.ShapeDtypeStruct(s, F32) for s...  5.03 us

profile of v2, /device:TPU:0, one launch (start us, length us, event | category | flops | bytes accessed | tf_op | source)
XLA Modules:
  0.0 122.2 jit_solution(15304658883529759661)
XLA Ops:
  0.6 116.4 %shard_map.143 = (f32[256,128]{1,0:T(8,128)}, f32[128,256]{1,0:T(8,128)}, f32[5,16,256]{2,1,0:T(8,128)}, f32[5,16]{1,0:T(8,128)}, f32[5,16]{1,0:T(8,128)}, /*ind...) custom-call(bf16[2048,128]{1,0:T(8,128)(2,1)} %bitcast.7, bf16[256,128]{1,0:T(8,128)(2,1)} %bitcast.8, ...), custom_call_target="tpu_custom_call" | custom-call | tf_op jit(solution)/shard_map/pallas_call | solution.py:1090
  117.0 5.0 %shard_map.144 = (f32[256,128]{1,0:T(8,128)}, f32[128,256]{1,0:T(8,128)}, f32[5,16,256]{2,1,0:T(8,128)}, f32[5,16]{1,0:T(8,128)}, f32[5,16]{1,0:T(8,128)}, /*ind...) custom-call(f32[256,128]{1,0:T(8,128)} %get-tuple-element.23.refs_0_, ...), custom_call_target="tpu_custom_call" | custom-call | tf_op jit(solution)/shard_map/pallas_call | solution.py:1110

commit v3 on v2

--- a/solution.py
+++ b/solution.py
@@ -228,6 +228,9 @@
 HALVES = 2
 SPAN = PIXELS // HALVES
 PIECES = [(b, half * SPAN) for b in ORDER for half in range(HALVES)]
+
+
+CROSS_FIRST = PIECES[-2:]
 
 
 def carries_pool(piece):
@@ -322,6 +325,8 @@
         "pt": vm((GROUPS, 16, 128), F32),
         "wp": vm((GROUPS, 5, 16, 256), BF16),
         "wpt": vm((256, 640), BF16),
+        "wps": vm((GROUPS, 2, 16, 128), BF16),
+        "pps": vm((2, GROUPS, 16, PIXELS), BF16),
         "xv": vm((2, 7, 128, PIXELS), BF16),
         "sl": vm((2, 4, GROUPS, 16, PIXELS), BF16),
         "flip": vm((128, 128), F32),
@@ -335,12 +340,13 @@
         "pi": vm((5, 128, 128), F32),
         "s1": vm((5, 128, 128), F32),
         "s2": vm((5, 128, 128), F32),
-        "pr": vm((2, GROUPS, 16, PIXELS), F32),
+        "pr": vm((2, GROUPS, 16, PIXELS), BF16),
         "dzp": vm((2, GROUPS, 16, PIXELS), F32),
         "dp": vm((2, GROUPS, 2, 16, PIXELS), BF16),
         "dpo": vm((GROUPS, 2, 16, 128), BF16),
         "d": vm((4, 2, GROUPS, 2, 16, PIXELS), BF16),
         "dwv": vm((28, 128, 256), BF16),
+        "rsum": vm((GROUPS, 2, 16, 128), F32),
         "fga": vm((128, PIXELS), F32),
         "fgv": vm((128, PIXELS), BF16),
         "pooled": vm((2, 128, 128), F32),
@@ -441,7 +447,7 @@
 
         def start(self):
             mine = self.slot(self.group(y, z))
-            for i in (1, 2, 3):
+            for i in (2, 1, 3):
                 send(mine, mine, self.nz + i - 1, zdev[i])
             send(mine, mine, self.ny, ydev)
             if self.across:
@@ -472,11 +478,17 @@
     g_og = Gather(lambda g: r.ogs.at[x, g], own_group, True)
     g_par = Gather(lambda g: r.pt.at[g], own_group, False)
     g_wp = Gather(lambda g: r.wp.at[g], own_group, False)
+    def sums_slot(piece, image):
+        return lambda g: r.g.at[piece[0], image, g, :, lanes_of(piece)]
+
     g_pre = {}
+    g_other = {}
+    n_cross = {}
     for piece in PIECES:
-        g_pre[piece] = Gather(
-            lambda g, b=piece[0], w=lanes_of(piece): r.g.at[b, x, g, :, w], pre_group, True
-        )
+        g_pre[piece] = Gather(sums_slot(piece, x), pre_group, piece not in CROSS_FIRST)
+        if piece in CROSS_FIRST:
+            g_other[piece] = Gather(sums_slot(piece, 1 - x), pre_group, False)
+            n_cross[piece] = new()
 
     mine = own_group(y, z)
     loads["og"].wait()
@@ -629,9 +641,13 @@
         if carries_pool(piece):
             r.g[b, x, g, :, PIXELS:WIDE] = encode_pair(extra)
         g_pre[piece].start()
-
-    def other_pre(piece):
-        return lambda g: r.g.at[piece[0], 1 - x, g, :, lanes_of(piece)]
+        if piece in CROSS_FIRST:
+            ref = sums_slot(piece, x)(g)
+            send(ref, ref, n_cross[piece], xdev)
+
+    def cross(piece):
+        arrived(sums_slot(piece, 1 - x)(pre_group(y, z)), n_cross[piece], xdev)
+        g_other[piece].start()
 
     shift_pairs = []
     lane_r = iota((128, 128), 0)
@@ -729,7 +745,7 @@
     g_par.start()
     g_wp.start()
     steps = len(PIECES)
-    for s in range(steps + 4):
+    for s in range(steps + 6):
         if s < steps:
             b = PIECES[s][0]
             if s % HALVES == 0:
@@ -739,35 +755,47 @@
             if s % HALVES == 0 and s // HALVES + 2 < len(ORDER):
                 prepare_weights(ORDER[s // HALVES + 2])
                 send_weights(ORDER[s // HALVES + 2])
-        if 1 <= s <= steps:
-            reduce_z_send(PIECES[s - 1])
-        if s == 1:
+        if s == 0:
             g_og.start()
+        if 0 <= s - 2 < steps:
+            reduce_z_send(PIECES[s - 2])
         if s == 2:
             g_par.forward_z()
             g_wp.forward_z()
             g_og.forward_z()
-        if 2 <= s <= steps + 1:
-            reduce_finish(PIECES[s - 2])
+        if 0 <= s - 3 < steps:
+            reduce_finish(PIECES[s - 3])
         if s == 4:
             g_par.forward_y()
             g_wp.forward_y()
-        if 3 <= s <= steps + 2:
-            g_pre[PIECES[s - 3]].forward_z()
-        if s >= 4:
-            g_pre[PIECES[s - 4]].forward_y()
-        if s == steps - 2:
+            g_og.forward_y()
+        if 0 <= s - 5 < steps:
+            g_pre[PIECES[s - 5]].forward_z()
+            if PIECES[s - 5] in CROSS_FIRST:
+                cross(PIECES[s - 5])
+        if 0 <= s - 6 < steps:
+            if PIECES[s - 6] in CROSS_FIRST:
+                g_other[PIECES[s - 6]].forward_z()
+            else:
+                g_pre[PIECES[s - 6]].forward_y()
+        if s == 6:
             place_shifted(r.feat, x)
-        if s == steps - 1:
+        if s == 7:
             arrived(r.foth, n_foth, xdev)
             place_shifted(r.foth, 1 - x)
-    g_og.forward_y()
 
     for b in range(5):
-        r.wpt[:, b * 128 : (b + 1) * 128] = dot_nt(eye, r.wp[:, b].reshape(128, 256)).astype(BF16)
+        flat = dot_nt(eye, r.wp[:, b].reshape(128, 256)).astype(BF16)
+        r.wps[...] = flat.reshape(GROUPS, 2, 16, 128)
+        r.wpt[0:128, b * 128 : (b + 1) * 128] = r.wps[:, k].reshape(128, 128)
+        r.wpt[128:256, b * 128 : (b + 1) * 128] = r.wps[:, 1 - k].reshape(128, 128)
 
     for piece in PIECES:
-        g_pre[piece].finish(other_pre(piece))
+        if piece in CROSS_FIRST:
+            g_pre[piece].forward_y()
+            g_other[piece].forward_y()
+        else:
+            g_pre[piece].finish(sums_slot(piece, 1 - x))
         if piece[1] == PIXELS - SPAN:
             branch_norm(piece[0])
 
@@ -782,16 +810,14 @@
     pool_out = dot(r.wpt[:, 512:640], pool_cols)
 
     n_pp = new(2)
-    pp_sent = []
     for image in range(2):
         column = pool_out[:, image : image + 1]
         for q in range(PIXELS // BLOCK):
             px = slice(q * BLOCK, (q + 1) * BLOCK)
             part = dot(r.wpt[:, 0:512], r.act[image, :, :, :, px].reshape(512, BLOCK)) + column
-            part = part.reshape(GROUPS, 2, 16, BLOCK)
-            r.acc[2 * image, :, :, px] = part[:, 0]
-            r.acc[2 * image + 1, :, :, px] = part[:, 1]
-        send(r.acc.at[2 * image + 1 - k], r.pr.at[image], n_pp + image, sibling, pp_sent)
+            r.acc[image, :, :, px] = part[0:128].reshape(GROUPS, 16, BLOCK)
+            r.pps[image, :, :, px] = part[128:256].astype(BF16).reshape(GROUPS, 16, BLOCK)
+        send(r.pps.at[image], r.pr.at[image], n_pp + image, sibling)
 
     for image in range(2):
         for b in range(4):
@@ -804,8 +830,8 @@
     def proj_sums(g, rows):
         s, q = zero_tile, zero_tile
         for image, px in tiles:
-            v = r.acc[2 * image + k, g, :, px] + r.pr[image, g, :, px]
-            r.pr[image, g, :, px] = v
+            v = r.acc[image, g, :, px] + r.pr[image, g, :, px].astype(F32)
+            r.acc[image, g, :, px] = v
             s = s + v
             q = q + v * v
         r.s1[4, rows] = s
@@ -818,7 +844,7 @@
         scale, base = r.pa[4, rows], r.pb[4, rows]
         s1, s2 = zero_tile, zero_tile
         for image, px in tiles:
-            v = r.pr[image, g, :, px]
+            v = r.acc[image, g, :, px]
             _, slope = act_and_slope(v * scale + base)
             dz = r.ogs[image, g, :, px].astype(F32) * slope
             r.dzp[image, g, :, px] = dz
@@ -834,35 +860,47 @@
 
         def proj_low(g, rows, image=image):
             scale, c1, c2 = r.pa[4, rows], r.c1[4, rows], r.c2[4, rows]
+            total = zero_tile
             for h in range(ROWS):
                 px = slice(h * 128, (h + 1) * 128)
-                low = scale * r.dzp[image, g, :, px] + (r.pr[image, g, :, px] * c2 + c1)
-                r.dp[image, g, k, :, px] = low.astype(BF16)
+                low = scale * r.dzp[image, g, :, px] + (r.acc[image, g, :, px] * c2 + c1)
+                low = low.astype(BF16)
+                r.dp[image, g, k, :, px] = low
+                total = total + low.astype(F32)
+            r.s1[image, rows] = total
 
         each_group(proj_low)
         ref = r.dp.at[image, :, k]
         send(ref, ref, n_dp + image, sibling)
 
+    n_rsum = new()
+    row_sums = jnp.where(lane128 == 0, lane_sum(r.s1[0]), 0.0)
+    row_sums = row_sums + jnp.where(lane128 == 1, lane_sum(r.s1[1]), 0.0)
+    r.rsum[:, k] = row_sums.reshape(GROUPS, 16, 128)
+    ref = r.rsum.at[:, k]
+    send(ref, ref, n_rsum, sibling)
+
     my_rows = pl.ds(pl.multiple_of(mine * 16, 16), 16)
     scale, base = r.pa[4, my_rows], r.pb[4, my_rows]
     for h in range(ROWS):
-        zed = r.pr[x, mine, :, h * 128 : (h + 1) * 128] * scale + base
+        zed = r.acc[x, mine, :, h * 128 : (h + 1) * 128] * scale + base
         r.out[pl.ds(h, 16, stride=16), :] = zed * sigmoid(zed)
 
     for image in range(2):
         arrived(r.dp.at[image, :, 1 - k], n_dp + image, sibling)
 
-    for copy in pp_sent:
-        copy.wait_send()
     n_d = {b: new(2) for b in ORDER}
 
+    def back_block(b, turn, image, q):
+        px = slice(q * 512, (q + 1) * 512)
+        dblock = r.dp[image, :, :, :, px].reshape(256, 512)
+        back = dot(r.wp[:, b].reshape(128, 256), dblock)
+        r.acc[2 * turn + image, :, :, px] = back.reshape(GROUPS, 16, 512)
+
     def branch_back(b, turn):
-        weights = r.wp[:, b].reshape(128, 256)
         for image in range(2):
             for q in range(PIXELS // 512):
-                px = slice(q * 512, (q + 1) * 512)
-                back = dot(weights, r.dp[image, :, :, :, px].reshape(256, 512))
-                r.acc[2 * turn + image, :, :, px] = back.reshape(GROUPS, 16, 512)
+                back_block(b, turn, image, q)
 
         def slope(g, rows):
             s1, s2 = zero_tile, zero_tile
@@ -943,17 +981,18 @@
                 r.fga[:, px] = total
 
     back_order = (1, 2, 3, 0)
-    branch_back(back_order[0], 0)
-
-    ones = jnp.ones((PIXELS, 128), BF16)
+    for n, b in enumerate(back_order):
+        branch_back(b, n % 2)
+    branch_grads(back_order[0], True, False)
+
+    arrived(r.rsum.at[:, 1 - k], n_rsum, sibling)
     wp4 = r.wp[:, 4].reshape(128, 256)
     dpo = jnp.zeros((128, 128), F32)
     dwp4 = jnp.zeros((16, 256), F32)
     lane16 = iota((16, 128), 1)
     for image in range(2):
-        dps = r.dp[image].reshape(256, PIXELS)
-        row_sums = dot(dps, ones)[:, 0:1]
-        pool_grad = lane_sum(dot(wp4, split_lanes(row_sums).astype(BF16)))
+        terms = split_lanes(r.rsum[...].reshape(256, 128)[:, image : image + 1]).astype(BF16)
+        pool_grad = lane_sum(dot(wp4, terms))
         pre = r.ppool[image][:, 0:1]
         _, slope = act_and_slope(pre)
         low = (pool_grad * slope).astype(BF16).astype(F32)
@@ -961,24 +1000,19 @@
             dpo = dpo + jnp.where(lane128 == lane, low, 0.0)
         mine_act, _ = act_and_slope(r.ppool[image, my_rows][:, 0:1])
         mine_act = mine_act.astype(BF16).astype(F32)
-        dwp4 = dwp4 + mine_act * dot_nt(jnp.ones((16, PIXELS), BF16), dps)
+        dwp4 = dwp4 + mine_act * dot_nt(jnp.ones((16, 128), BF16), terms)
     r.dwproj[4] = dwp4
     r.dpo[:, k] = dpo.astype(BF16).reshape(GROUPS, 16, 128)
     n_dpo = new()
     ref = r.dpo.at[:, k]
     send(ref, ref, n_dpo, sibling)
 
-    branch_back(back_order[1], 1)
-    branch_grads(back_order[0], True, False)
-    branch_back(back_order[2], 0)
+    branch_grads(back_order[1], False, False)
 
     dwp = jnp.zeros((64, 256), F32)
     for image in range(2):
         dwp = dwp + dot_nt(r.ao[image].reshape(64, PIXELS), r.dp[image].reshape(256, PIXELS))
     r.dwproj[0:4] = dwp.reshape(4, 16, 256)
-
-    branch_grads(back_order[1], False, False)
-    branch_back(back_order[3], 1)
 
     tile = jnp.zeros((16, 128), F32)
     for b in range(5):

time: 122 us -> 115 us (0.943)
  Pallas kernels: 121 us -> 114 us
    pallas_call x1, Pallas kernels: 116 us -> 109 us  [fused(): pl.pallas_call(head_kernel, out_shape=shapes, in_specs=[hbm] * len(INPUTS...]
where the time goes in v3:
time: 115 us
  Pallas kernels  114 us (99%)
    pallas_call x1, Pallas kernels, fused(): pl.pallas_call(head_kernel, out_shape=shapes, in_specs=[hbm] * len(INPUTS...  109 us
    pallas_call x1, Pallas kernels, fused(): pl.pallas_call(copy_kernel, out_shape=[jax.ShapeDtypeStruct(s, F32) for s...  5.03 us

profile of v3, /device:TPU:0, one launch (start us, length us, event | category | flops | bytes accessed | tf_op | source)
XLA Modules:
  0.0 115.0 jit_solution(5571841354004757038)
XLA Ops:
  0.6 109.2 %shard_map.143 = (f32[256,128]{1,0:T(8,128)}, f32[128,256]{1,0:T(8,128)}, f32[5,16,256]{2,1,0:T(8,128)}, f32[5,16]{1,0:T(8,128)}, f32[5,16]{1,0:T(8,128)}, /*ind...) custom-call(bf16[2048,128]{1,0:T(8,128)(2,1)} %bitcast.7, bf16[256,128]{1,0:T(8,128)(2,1)} %bitcast.8, ...), custom_call_target="tpu_custom_call" | custom-call | tf_op jit(solution)/shard_map/pallas_call | solution.py:1124
  109.8 5.0 %shard_map.144 = (f32[256,128]{1,0:T(8,128)}, f32[128,256]{1,0:T(8,128)}, f32[5,16,256]{2,1,0:T(8,128)}, f32[5,16]{1,0:T(8,128)}, f32[5,16]{1,0:T(8,128)}, /*ind...) custom-call(f32[256,128]{1,0:T(8,128)} %get-tuple-element.23.refs_0_, ...), custom_call_target="tpu_custom_call" | custom-call | tf_op jit(solution)/shard_map/pallas_call | solution.py:1144

commit v4 on v3

--- a/solution.py
+++ b/solution.py
@@ -301,6 +301,11 @@
 def scratch_table(sems):
     vm = pltpu.VMEM
     return {
+        "outv": vm((256, 128), F32),
+        "dwpoolv": vm((128, 256), F32),
+        "dwprojv": vm((5, 16, 256), F32),
+        "dgainsv": vm((5, 16), F32),
+        "dbiasesv": vm((5, 16), F32),
         "feat": vm((2048, 128), BF16),
         "og": vm((256, 128), BF16),
         "w1": vm((128, 256), BF16),
@@ -309,9 +314,7 @@
         "wproj": vm((5, 16, 256), BF16),
         "gains": vm((5, 16), F32),
         "biases": vm((5, 16), F32),
-        "fsib": vm((2048, 128), BF16),
-        "foth": vm((2048, 128), BF16),
-        "x": vm((256, PIXELS), BF16),
+        "xsib": vm((128, PIXELS), BF16),
         "tw": vm((NSLOTS, GROUPS, 2, 16, 128), BF16),
         "lw": vm((NSLOTS, GROUPS, 16, 256), BF16),
         "acc": vm((4, GROUPS, 16, PIXELS), F32),
@@ -536,31 +539,31 @@
         lo, hi = SPANS[b]
         arrived(r.lw.at[pl.ds(lo, hi - lo), :, :, pl.ds(128, 128)], n_w[b], sibling)
 
-    def place(ref, base):
-        for block in range(8):
-            t = permuted(ref, block)
-            for h in range(ROWS):
-                r.x[base + block * 16 : base + (block + 1) * 16, h * 128 : (h + 1) * 128] = t[
-                    h * 16 : (h + 1) * 16
-                ]
-
     for name in ("w1", "wpool", "feat"):
         loads[name].wait()
+    for block in range(8):
+        t = permuted(r.feat, block)
+        for h in range(ROWS):
+            px = slice(h * 128, (h + 1) * 128)
+            r.xv[x, 0, block * 16 : (block + 1) * 16, px] = t[h * 16 : (h + 1) * 16]
     prepare_weights(0)
-    place(r.feat, 0)
     loads["wa"].wait()
     prepare_weights(ORDER[1])
 
     pl.semaphore_wait(barrier, len(partners))
 
-    n_feat = new()
+    n_feat = new(2)
     n_foth = new()
-    send(r.feat, r.fsib, n_feat, sibling)
+    halves = [pl.ds(0, PIXELS // 2), pl.ds(PIXELS // 2, PIXELS // 2)]
     send_weights(0)
+    for n in range(2):
+        send(r.xv.at[x, 0, :, halves[n]], r.xsib.at[:, halves[n]], n_feat + n, sibling)
     send_weights(ORDER[1])
-    send(r.feat, r.foth, n_foth, xdev)
-    arrived(r.fsib, n_feat, sibling)
-    place(r.fsib, 128)
+    send(r.xv.at[x, 0], r.xv.at[x, 0], n_foth, xdev)
+    arrived(r.xsib.at[:, halves[0]], n_feat, sibling)
+
+    def features_at(px):
+        return jnp.concatenate([r.xv[x, 0, :, px], r.xsib[:, px]], axis=0)
 
     def convolve(piece):
         b = piece[0]
@@ -574,7 +577,7 @@
                 slot = SLOTS[(b, i)]
                 count = 1 if b == 0 else 3
                 weights = r.lw[slot : slot + count].reshape(count * 128, 256)
-                part = dot(weights, r.x[:, source * BLOCK : (source + 1) * BLOCK])
+                part = dot(weights, features_at(slice(source * BLOCK, (source + 1) * BLOCK)))
                 total = part if total is None else total + part
             if b:
                 rate = atrous_rates[b - 1]
@@ -587,7 +590,7 @@
         if carries_pool(piece):
             pooled = jnp.zeros((256, 128), F32)
             for h in range(ROWS):
-                pooled = pooled + r.x[:, h * 128 : (h + 1) * 128].astype(F32)
+                pooled = pooled + features_at(slice(h * 128, (h + 1) * 128)).astype(F32)
             column = lane_sum(pooled) / PIXELS
             r.pooled[x] = jnp.broadcast_to(column[0:128], (128, 128))
             terms = split_lanes(column).astype(BF16)
@@ -664,28 +667,19 @@
         copy.start()
         local.append(copy)
 
-    def place_shifted(ref, image):
-        for block in range(8):
-            t = permuted(ref, block)
-            rows = slice(block * 16, (block + 1) * 16)
+    def place_shifted(image):
+        for h in range(ROWS):
+            px = slice(h * 128, (h + 1) * 128)
             for a in range(3):
-                both = dot(t, shift_pairs[a]).astype(BF16)
-                for h in range(ROWS):
-                    px = slice(h * 128, (h + 1) * 128)
-                    hc = slice(h * 16, (h + 1) * 16)
-                    if a == 0:
-                        r.xv[image, 0, rows, px] = t[hc]
-                    r.xv[image, 1 + 2 * a, rows, px] = both[hc, 0:128]
-                    r.xv[image, 2 + 2 * a, rows, px] = both[hc, 128:256]
+                both = dot(r.xv[image, 0, :, px], shift_pairs[a]).astype(BF16)
+                r.xv[image, 1 + 2 * a, :, px] = both[:, 0:128]
+                r.xv[image, 2 + 2 * a, :, px] = both[:, 128:256]
 
     count = float(2 * PIXELS)
 
     def each_group(body):
-        def step(g, _):
-            body(g, pl.ds(pl.multiple_of(g * 16, 16), 16))
-            return 0
-
-        lax.fori_loop(0, GROUPS, step, 0)
+        for g in range(GROUPS):
+            body(g, pl.ds(g * 16, 16))
 
     tiles = [(image, slice(h * 128, (h + 1) * 128)) for image in range(2) for h in range(ROWS)]
     zero_tile = jnp.zeros((16, 128), F32)
@@ -751,6 +745,8 @@
             if s % HALVES == 0:
                 wait_weights(b)
             convolve(PIECES[s])
+            if s == 0:
+                arrived(r.xsib.at[:, halves[1]], n_feat + 1, sibling)
             reduce_y_send(PIECES[s])
             if s % HALVES == 0 and s // HALVES + 2 < len(ORDER):
                 prepare_weights(ORDER[s // HALVES + 2])
@@ -779,10 +775,14 @@
             else:
                 g_pre[PIECES[s - 6]].forward_y()
         if s == 6:
-            place_shifted(r.feat, x)
+            place_shifted(x)
         if s == 7:
-            arrived(r.foth, n_foth, xdev)
-            place_shifted(r.foth, 1 - x)
+            arrived(r.xv.at[1 - x, 0], n_foth, xdev)
+            place_shifted(1 - x)
+            pooled = jnp.zeros((128, 128), F32)
+            for h in range(ROWS):
+                pooled = pooled + r.xv[1 - x, 0, :, h * 128 : (h + 1) * 128].astype(F32)
+            r.pooled[1 - x] = spread_lanes(lane_sum(pooled) / PIXELS)
 
     for b in range(5):
         flat = dot_nt(eye, r.wp[:, b].reshape(128, 256)).astype(BF16)
@@ -884,7 +884,8 @@
     scale, base = r.pa[4, my_rows], r.pb[4, my_rows]
     for h in range(ROWS):
         zed = r.acc[x, mine, :, h * 128 : (h + 1) * 128] * scale + base
-        r.out[pl.ds(h, 16, stride=16), :] = zed * sigmoid(zed)
+        r.outv[pl.ds(h, 16, stride=16), :] = zed * sigmoid(zed)
+    keep(r.outv, r.out)
 
     for image in range(2):
         arrived(r.dp.at[image, :, 1 - k], n_dp + image, sibling)
@@ -896,6 +897,15 @@
         dblock = r.dp[image, :, :, :, px].reshape(256, 512)
         back = dot(r.wp[:, b].reshape(128, 256), dblock)
         r.acc[2 * turn + image, :, :, px] = back.reshape(GROUPS, 16, 512)
+
+    back_order = (1, 2, 3, 0)
+
+    dwp = [jnp.zeros((64, 256), F32)]
+
+    def proj_weights(image, q):
+        px = slice(q * 512, (q + 1) * 512)
+        acts = r.ao[image, :, :, px].reshape(64, 512)
+        dwp[0] = dwp[0] + dot_nt(acts, r.dp[image, :, :, :, px].reshape(256, 512))
 
     def branch_back(b, turn):
         for image in range(2):
@@ -911,6 +921,8 @@
                 s2 = s2 + dz * r.g[b, image, g, :, px].astype(F32)
             r.s1[b, rows] = s1
             r.s2[b, rows] = s2
+            if b == back_order[0]:
+                proj_weights(g // 4, g % 4)
 
         each_group(slope)
         grad_params(b)
@@ -980,11 +992,6 @@
             else:
                 r.fga[:, px] = total
 
-    back_order = (1, 2, 3, 0)
-    for n, b in enumerate(back_order):
-        branch_back(b, n % 2)
-    branch_grads(back_order[0], True, False)
-
     arrived(r.rsum.at[:, 1 - k], n_rsum, sibling)
     wp4 = r.wp[:, 4].reshape(128, 256)
     dpo = jnp.zeros((128, 128), F32)
@@ -1001,18 +1008,19 @@
         mine_act, _ = act_and_slope(r.ppool[image, my_rows][:, 0:1])
         mine_act = mine_act.astype(BF16).astype(F32)
         dwp4 = dwp4 + mine_act * dot_nt(jnp.ones((16, 128), BF16), terms)
-    r.dwproj[4] = dwp4
+    r.dwprojv[4] = dwp4
     r.dpo[:, k] = dpo.astype(BF16).reshape(GROUPS, 16, 128)
     n_dpo = new()
     ref = r.dpo.at[:, k]
     send(ref, ref, n_dpo, sibling)
 
+    for n, b in enumerate(back_order):
+        branch_back(b, n % 2)
+        if n == 0:
+            r.dwprojv[0:4] = dwp[0].reshape(4, 16, 256)
+            keep(r.dwprojv, r.dwproj)
+    branch_grads(back_order[0], True, False)
     branch_grads(back_order[1], False, False)
-
-    dwp = jnp.zeros((64, 256), F32)
-    for image in range(2):
-        dwp = dwp + dot_nt(r.ao[image].reshape(64, PIXELS), r.dp[image].reshape(256, PIXELS))
-    r.dwproj[0:4] = dwp.reshape(4, 16, 256)
 
     tile = jnp.zeros((16, 128), F32)
     for b in range(5):
@@ -1020,21 +1028,20 @@
         tile = tile + jnp.where(lane16 == 8 + b, r.s1[b, my_rows], 0.0)
     r.flip[0:16, :] = tile
     flipped = r.flip[...].T
-    r.dgains[...] = flipped[0:5, 0:16]
-    r.dbiases[...] = flipped[8:13, 0:16]
+    r.dgainsv[...] = flipped[0:5, 0:16]
+    r.dbiasesv[...] = flipped[8:13, 0:16]
+    keep(r.dgainsv, r.dgains)
+    keep(r.dbiasesv, r.dbiases)
 
     branch_grads(back_order[2], False, False)
 
-    pooled = jnp.zeros((128, 128), F32)
-    for h in range(ROWS):
-        pooled = pooled + r.xv[1 - x, 0, :, h * 128 : (h + 1) * 128].astype(F32)
-    r.pooled[1 - x] = spread_lanes(lane_sum(pooled) / PIXELS)
     arrived(r.dpo.at[:, 1 - k], n_dpo, sibling)
     dpo = r.dpo[...].reshape(256, 128)
     pooled = jnp.zeros((128, 128), F32)
     for image in range(2):
         pooled = pooled + split_lanes(r.pooled[image][:, 0:1], (image, image + 2, image + 4))
-    r.dwpool[...] = dot_nt(pooled.astype(BF16), dpo)
+    r.dwpoolv[...] = dot_nt(pooled.astype(BF16), dpo)
+    keep(r.dwpoolv, r.dwpool)
     spread = dot(r.wpool[...], dpo)
     fg_pool = lane_sum(jnp.where(lane128 == x, spread, 0.0)) / PIXELS
 
@@ -1125,7 +1132,7 @@
         head_kernel,
         out_shape=shapes,
         in_specs=[hbm] * len(INPUTS),
-        out_specs=[vmem] * 5 + [hbm] * 2,
+        out_specs=[hbm] * len(OUTPUTS),
         scratch_shapes=list(scratch_table(NSEMS).values()),
         compiler_params=pltpu.CompilerParams(
             collective_id=0, has_side_effects=True, vmem_limit_bytes=64 * 2**20

time: 115 us -> 112 us (0.974)
  Pallas kernels: 114 us -> 111 us
    pallas_call x1, Pallas kernels: 109 us -> 106 us  [fused(): pl.pallas_call(head_kernel, out_shape=shapes, in_specs=[hbm] * len(INPUTS...]
where the time goes in v4:
time: 112 us; the launch traced here: 111 us
  Pallas kernels  111 us (99%)
    pallas_call x1, Pallas kernels, fused(): pl.pallas_call(head_kernel, out_shape=shapes, in_specs=[hbm] * len(INPUTS...  106 us
    pallas_call x1, Pallas kernels, fused(): pl.pallas_call(copy_kernel, out_shape=[jax.ShapeDtypeStruct(s, F32) for s...  5.03 us

profile of v4, /device:TPU:0, one launch (start us, length us, event | category | flops | bytes accessed | tf_op | source)
XLA Modules:
  0.0 111.5 jit_solution(18253054651764129130)
XLA Ops:
  0.6 105.6 %shard_map.143 = (f32[256,128]{1,0:T(8,128)}, f32[128,256]{1,0:T(8,128)}, f32[5,16,256]{2,1,0:T(8,128)}, f32[5,16]{1,0:T(8,128)}, f32[5,16]{1,0:T(8,128)}, /*ind...) custom-call(bf16[2048,128]{1,0:T(8,128)(2,1)} %bitcast.7, bf16[256,128]{1,0:T(8,128)(2,1)} %bitcast.8, ...), custom_call_target="tpu_custom_call" | custom-call | tf_op jit(solution)/shard_map/pallas_call | solution.py:1131
  106.3 5.0 %shard_map.144 = (f32[256,128]{1,0:T(8,128)}, f32[128,256]{1,0:T(8,128)}, f32[5,16,256]{2,1,0:T(8,128)}, f32[5,16]{1,0:T(8,128)}, f32[5,16]{1,0:T(8,128)}, /*ind...) custom-call(f32[256,128]{1,0:T(8,128)} %get-tuple-element.23.refs_0_, ...), custom_call_target="tpu_custom_call" | custom-call | tf_op jit(solution)/shard_map/pallas_call | solution.py:1151

commit v5 on v4

--- a/solution.py
+++ b/solution.py
@@ -329,6 +329,10 @@
         "wp": vm((GROUPS, 5, 16, 256), BF16),
         "wpt": vm((256, 640), BF16),
         "wps": vm((GROUPS, 2, 16, 128), BF16),
+        "pools": vm((128, 128), F32),
+        "poolo": vm((128, 128), F32),
+        "poolr": vm((128, 128), F32),
+        "pcol": vm((2, 128, 128), F32),
         "pps": vm((2, GROUPS, 16, PIXELS), BF16),
         "xv": vm((2, 7, 128, PIXELS), BF16),
         "sl": vm((2, 4, GROUPS, 16, PIXELS), BF16),
@@ -546,6 +550,10 @@
         for h in range(ROWS):
             px = slice(h * 128, (h + 1) * 128)
             r.xv[x, 0, block * 16 : (block + 1) * 16, px] = t[h * 16 : (h + 1) * 16]
+    pooled = jnp.zeros((128, 128), F32)
+    for h in range(ROWS):
+        pooled = pooled + r.xv[x, 0, :, h * 128 : (h + 1) * 128].astype(F32)
+    r.pooled[x] = jnp.broadcast_to(lane_sum(pooled) / PIXELS, (128, 128))
     prepare_weights(0)
     loads["wa"].wait()
     prepare_weights(ORDER[1])
@@ -588,11 +596,10 @@
                 )
             r.acc[b, :, :, px] = total.reshape(GROUPS, 16, BLOCK)
         if carries_pool(piece):
-            pooled = jnp.zeros((256, 128), F32)
+            pooled = jnp.zeros((128, 128), F32)
             for h in range(ROWS):
-                pooled = pooled + features_at(slice(h * 128, (h + 1) * 128)).astype(F32)
-            column = lane_sum(pooled) / PIXELS
-            r.pooled[x] = jnp.broadcast_to(column[0:128], (128, 128))
+                pooled = pooled + r.xsib[:, h * 128 : (h + 1) * 128].astype(F32)
+            column = jnp.concatenate([r.pooled[x][:, 0:1], lane_sum(pooled) / PIXELS], axis=0)
             terms = split_lanes(column).astype(BF16)
             slot = SLOTS["pool"]
             sums = lane_sum(dot(r.lw[slot].reshape(128, 256), terms))
@@ -677,6 +684,13 @@
 
     count = float(2 * PIXELS)
 
+    def each_group_loop(body):
+        def step(g, _):
+            body(g, pl.ds(pl.multiple_of(g * 16, 16), 16))
+            return 0
+
+        lax.fori_loop(0, GROUPS, step, 0)
+
     def each_group(body):
         for g in range(GROUPS):
             body(g, pl.ds(g * 16, 16))
@@ -714,7 +728,7 @@
         act = zed * sg
         return act, sg + act * (0.5 - u)
 
-    def branch_norm(b):
+    def branch_norm(b, each_group):
         def sums(g, rows):
             s, q = zero_tile, zero_tile
             for image, px in tiles:
@@ -735,6 +749,40 @@
                 r.sl[image, b, g, :, px] = slope.astype(BF16)
 
         each_group(apply)
+
+    lane128 = iota((128, 128), 1)
+    n_pool = new()
+
+    def pool_part():
+        pool_cols = jnp.zeros((128, 128), F32)
+        for image in range(2):
+            pre = decode_pair(r.g[0, image, :, :, PIXELS:WIDE]).reshape(128, 128)
+            r.ppool[image] = pre
+            pool_cols = pool_cols + jnp.where(lane128 == image, pre * sigmoid(pre), 0.0)
+        pool_cols = pool_cols.astype(BF16)
+        pool_out = dot(r.wpt[:, 512:640], pool_cols)
+        r.poolo[...] = pool_out[0:128]
+
+        r.pools[...] = pool_out[128:256]
+        send(r.pools, r.poolr, n_pool, sibling)
+
+    def finish_branch(b, groups):
+        for piece in PIECES:
+            if piece[0] != b:
+                continue
+            if piece in CROSS_FIRST:
+                g_pre[piece].forward_y()
+                g_other[piece].forward_y()
+            else:
+                g_pre[piece].finish(sums_slot(piece, 1 - x))
+        branch_norm(b, groups)
+
+    def projection_weights():
+        for b in range(5):
+            flat = dot_nt(eye, r.wp[:, b].reshape(128, 256)).astype(BF16)
+            r.wps[...] = flat.reshape(GROUPS, 2, 16, 128)
+            r.wpt[0:128, b * 128 : (b + 1) * 128] = r.wps[:, k].reshape(128, 128)
+            r.wpt[128:256, b * 128 : (b + 1) * 128] = r.wps[:, 1 - k].reshape(128, 128)
 
     g_par.start()
     g_wp.start()
@@ -765,6 +813,8 @@
             g_par.forward_y()
             g_wp.forward_y()
             g_og.forward_y()
+        if s == 8:
+            projection_weights()
         if 0 <= s - 5 < steps:
             g_pre[PIECES[s - 5]].forward_z()
             if PIECES[s - 5] in CROSS_FIRST:
@@ -783,38 +833,20 @@
             for h in range(ROWS):
                 pooled = pooled + r.xv[1 - x, 0, :, h * 128 : (h + 1) * 128].astype(F32)
             r.pooled[1 - x] = spread_lanes(lane_sum(pooled) / PIXELS)
-
-    for b in range(5):
-        flat = dot_nt(eye, r.wp[:, b].reshape(128, 256)).astype(BF16)
-        r.wps[...] = flat.reshape(GROUPS, 2, 16, 128)
-        r.wpt[0:128, b * 128 : (b + 1) * 128] = r.wps[:, k].reshape(128, 128)
-        r.wpt[128:256, b * 128 : (b + 1) * 128] = r.wps[:, 1 - k].reshape(128, 128)
-
-    for piece in PIECES:
-        if piece in CROSS_FIRST:
-            g_pre[piece].forward_y()
-            g_other[piece].forward_y()
-        else:
-            g_pre[piece].finish(sums_slot(piece, 1 - x))
-        if piece[1] == PIXELS - SPAN:
-            branch_norm(piece[0])
-
-    pool_act = []
-    lane128 = iota((128, 128), 1)
-    pool_cols = jnp.zeros((128, 128), F32)
-    for image in range(2):
-        pre = decode_pair(r.g[0, image, :, :, PIXELS:WIDE]).reshape(128, 128)
-        r.ppool[image] = pre
-        pool_cols = pool_cols + jnp.where(lane128 == image, pre * sigmoid(pre), 0.0)
-    pool_cols = pool_cols.astype(BF16)
-    pool_out = dot(r.wpt[:, 512:640], pool_cols)
+        if s == 11:
+            finish_branch(ORDER[0], each_group_loop)
+            pool_part()
+        if s == 12:
+            finish_branch(ORDER[1], each_group_loop)
+
+    for b in ORDER[2:]:
+        finish_branch(b, each_group)
 
     n_pp = new(2)
     for image in range(2):
-        column = pool_out[:, image : image + 1]
         for q in range(PIXELS // BLOCK):
             px = slice(q * BLOCK, (q + 1) * BLOCK)
-            part = dot(r.wpt[:, 0:512], r.act[image, :, :, :, px].reshape(512, BLOCK)) + column
+            part = dot(r.wpt[:, 0:512], r.act[image, :, :, :, px].reshape(512, BLOCK))
             r.acc[image, :, :, px] = part[0:128].reshape(GROUPS, 16, BLOCK)
             r.pps[image, :, :, px] = part[128:256].astype(BF16).reshape(GROUPS, 16, BLOCK)
         send(r.pps.at[image], r.pr.at[image], n_pp + image, sibling)
@@ -826,11 +858,16 @@
     g_og.finish(lambda g: r.ogs.at[1 - x, g])
     for image in range(2):
         arrived(r.pr.at[image], n_pp + image, sibling)
+
+    arrived(r.poolr, n_pool, sibling)
+    for image in range(2):
+        r.pcol[image] = spread_lanes((r.poolo[...] + r.poolr[...])[:, image : image + 1])
 
     def proj_sums(g, rows):
         s, q = zero_tile, zero_tile
         for image, px in tiles:
             v = r.acc[image, g, :, px] + r.pr[image, g, :, px].astype(F32)
+            v = v + r.pcol[image, rows]
             r.acc[image, g, :, px] = v
             s = s + v
             q = q + v * v
@@ -889,6 +926,7 @@
 
     for image in range(2):
         arrived(r.dp.at[image, :, 1 - k], n_dp + image, sibling)
+    arrived(r.rsum.at[:, 1 - k], n_rsum, sibling)
 
     n_d = {b: new(2) for b in ORDER}
 
@@ -940,9 +978,12 @@
             there = r.d.at[b, image, :, k]
             send(there, there, n_d[b] + image, sibling)
 
+    def wait_grads(*branches):
+        for b in branches:
+            for image in range(2):
+                arrived(r.d.at[b, image, :, 1 - k], n_d[b] + image, sibling)
+
     def branch_grads(b, first_branch, last_branch):
-        for image in range(2):
-            arrived(r.d.at[b, image, :, 1 - k], n_d[b] + image, sibling)
         planes = (2 * b - 1, 0, 2 * b)
         for i, offset in branch_rows(b):
             first, last = max(0, -offset), min(ROWS, ROWS - offset)
@@ -992,7 +1033,6 @@
             else:
                 r.fga[:, px] = total
 
-    arrived(r.rsum.at[:, 1 - k], n_rsum, sibling)
     wp4 = r.wp[:, 4].reshape(128, 256)
     dpo = jnp.zeros((128, 128), F32)
     dwp4 = jnp.zeros((16, 256), F32)
@@ -1011,15 +1051,16 @@
     r.dwprojv[4] = dwp4
     r.dpo[:, k] = dpo.astype(BF16).reshape(GROUPS, 16, 128)
     n_dpo = new()
-    ref = r.dpo.at[:, k]
-    send(ref, ref, n_dpo, sibling)
-
     for n, b in enumerate(back_order):
         branch_back(b, n % 2)
         if n == 0:
+            ref = r.dpo.at[:, k]
+            send(ref, ref, n_dpo, sibling)
             r.dwprojv[0:4] = dwp[0].reshape(4, 16, 256)
             keep(r.dwprojv, r.dwproj)
+    wait_grads(back_order[0])
     branch_grads(back_order[0], True, False)
+    wait_grads(*back_order[1:])
     branch_grads(back_order[1], False, False)
 
     tile = jnp.zeros((16, 128), F32)

time: 112 us -> 110 us (0.982)
  Pallas kernels: 111 us -> 109 us
    pallas_call x1, Pallas kernels: 106 us -> 104 us  [fused(): pl.pallas_call(head_kernel, out_shape=shapes, in_specs=[hbm] * len(INPUTS...]
where the time goes in v5:
time: 110 us
  Pallas kernels  109 us (99%)
    pallas_call x1, Pallas kernels, fused(): pl.pallas_call(head_kernel, out_shape=shapes, in_specs=[hbm] * len(INPUTS...  104 us
    pallas_call x1, Pallas kernels, fused(): pl.pallas_call(copy_kernel, out_shape=[jax.ShapeDtypeStruct(s, F32) for s...  5.03 us

profile of v5, /device:TPU:0, one launch (start us, length us, event | category | flops | bytes accessed | tf_op | source)
XLA Modules:
  0.0 109.6 jit_solution(9247326568451790238)
XLA Ops:
  0.6 103.8 %shard_map.143 = (f32[256,128]{1,0:T(8,128)}, f32[128,256]{1,0:T(8,128)}, f32[5,16,256]{2,1,0:T(8,128)}, f32[5,16]{1,0:T(8,128)}, f32[5,16]{1,0:T(8,128)}, /*ind...) custom-call(bf16[2048,128]{1,0:T(8,128)(2,1)} %bitcast.7, bf16[256,128]{1,0:T(8,128)(2,1)} %bitcast.8, ...), custom_call_target="tpu_custom_call" | custom-call | tf_op jit(solution)/shard_map/pallas_call | solution.py:1172
  104.4 5.0 %shard_map.144 = (f32[256,128]{1,0:T(8,128)}, f32[128,256]{1,0:T(8,128)}, f32[5,16,256]{2,1,0:T(8,128)}, f32[5,16]{1,0:T(8,128)}, f32[5,16]{1,0:T(8,128)}, /*ind...) custom-call(f32[256,128]{1,0:T(8,128)} %get-tuple-element.23.refs_0_, ...), custom_call_target="tpu_custom_call" | custom-call | tf_op jit(solution)/shard_map/pallas_call | solution.py:1192

commit v6 on v5

--- a/solution.py
+++ b/solution.py
@@ -566,8 +566,11 @@
     send_weights(0)
     for n in range(2):
         send(r.xv.at[x, 0, :, halves[n]], r.xsib.at[:, halves[n]], n_feat + n, sibling)
+    g_og.start()
     send_weights(ORDER[1])
     send(r.xv.at[x, 0], r.xv.at[x, 0], n_foth, xdev)
+    g_par.start()
+    g_wp.start()
     arrived(r.xsib.at[:, halves[0]], n_feat, sibling)
 
     def features_at(px):
@@ -784,10 +787,8 @@
             r.wpt[0:128, b * 128 : (b + 1) * 128] = r.wps[:, k].reshape(128, 128)
             r.wpt[128:256, b * 128 : (b + 1) * 128] = r.wps[:, 1 - k].reshape(128, 128)
 
-    g_par.start()
-    g_wp.start()
     steps = len(PIECES)
-    for s in range(steps + 6):
+    for s in range(steps + 5):
         if s < steps:
             b = PIECES[s][0]
             if s % HALVES == 0:
@@ -799,31 +800,29 @@
             if s % HALVES == 0 and s // HALVES + 2 < len(ORDER):
                 prepare_weights(ORDER[s // HALVES + 2])
                 send_weights(ORDER[s // HALVES + 2])
-        if s == 0:
-            g_og.start()
-        if 0 <= s - 2 < steps:
-            reduce_z_send(PIECES[s - 2])
+        if 0 <= s - 1 < steps:
+            reduce_z_send(PIECES[s - 1])
         if s == 2:
             g_par.forward_z()
             g_wp.forward_z()
             g_og.forward_z()
-        if 0 <= s - 3 < steps:
-            reduce_finish(PIECES[s - 3])
-        if s == 4:
+        if 0 <= s - 2 < steps:
+            reduce_finish(PIECES[s - 2])
+        if s == 3:
             g_par.forward_y()
             g_wp.forward_y()
             g_og.forward_y()
         if s == 8:
             projection_weights()
+        if 0 <= s - 3 < steps:
+            g_pre[PIECES[s - 3]].forward_z()
+            if PIECES[s - 3] in CROSS_FIRST:
+                cross(PIECES[s - 3])
         if 0 <= s - 5 < steps:
-            g_pre[PIECES[s - 5]].forward_z()
             if PIECES[s - 5] in CROSS_FIRST:
-                cross(PIECES[s - 5])
-        if 0 <= s - 6 < steps:
-            if PIECES[s - 6] in CROSS_FIRST:
-                g_other[PIECES[s - 6]].forward_z()
+                g_other[PIECES[s - 5]].forward_z()
             else:
-                g_pre[PIECES[s - 6]].forward_y()
+                g_pre[PIECES[s - 5]].forward_y()
         if s == 6:
             place_shifted(x)
         if s == 7:
@@ -945,7 +944,7 @@
         acts = r.ao[image, :, :, px].reshape(64, 512)
         dwp[0] = dwp[0] + dot_nt(acts, r.dp[image, :, :, :, px].reshape(256, 512))
 
-    def branch_back(b, turn):
+    def branch_slope(b, turn):
         for image in range(2):
             for q in range(PIXELS // 512):
                 back_block(b, turn, image, q)
@@ -963,6 +962,8 @@
                 proj_weights(g // 4, g % 4)
 
         each_group(slope)
+
+    def branch_low(b, turn):
         grad_params(b)
         for image in range(2):
 
@@ -1051,8 +1052,11 @@
     r.dwprojv[4] = dwp4
     r.dpo[:, k] = dpo.astype(BF16).reshape(GROUPS, 16, 128)
     n_dpo = new()
+    branch_slope(back_order[0], 0)
     for n, b in enumerate(back_order):
-        branch_back(b, n % 2)
+        if n + 1 < len(back_order):
+            branch_slope(back_order[n + 1], (n + 1) % 2)
+        branch_low(b, n % 2)
         if n == 0:
             ref = r.dpo.at[:, k]
             send(ref, ref, n_dpo, sibling)

time: 110 us -> 108 us (0.982)
  Pallas kernels: 109 us -> 106 us
    pallas_call x1, Pallas kernels: 104 us -> 101 us  [fused(): pl.pallas_call(head_kernel, out_shape=shapes, in_specs=[hbm] * len(INPUTS...]
where the time goes in v6:
time: 108 us; the launch traced here: 107 us
  Pallas kernels  106 us (98%)
    pallas_call x1, Pallas kernels, fused(): pl.pallas_call(head_kernel, out_shape=shapes, in_specs=[hbm] * len(INPUTS...  101 us
    pallas_call x1, Pallas kernels, fused(): pl.pallas_call(copy_kernel, out_shape=[jax.ShapeDtypeStruct(s, F32) for s...  5.03 us

profile of v6, /device:TPU:0, one launch (start us, length us, event | category | flops | bytes accessed | tf_op | source)
XLA Modules:
  0.0 107.2 jit_solution(200399191467800578)
XLA Ops:
  0.6 101.3 %shard_map.143 = (f32[256,128]{1,0:T(8,128)}, f32[128,256]{1,0:T(8,128)}, f32[5,16,256]{2,1,0:T(8,128)}, f32[5,16]{1,0:T(8,128)}, f32[5,16]{1,0:T(8,128)}, /*ind...) custom-call(bf16[2048,128]{1,0:T(8,128)(2,1)} %bitcast.7, bf16[256,128]{1,0:T(8,128)(2,1)} %bitcast.8, ...), custom_call_target="tpu_custom_call" | custom-call | tf_op jit(solution)/shard_map/pallas_call | solution.py:1176
  102.0 5.0 %shard_map.144 = (f32[256,128]{1,0:T(8,128)}, f32[128,256]{1,0:T(8,128)}, f32[5,16,256]{2,1,0:T(8,128)}, f32[5,16]{1,0:T(8,128)}, f32[5,16]{1,0:T(8,128)}, /*ind...) custom-call(f32[256,128]{1,0:T(8,128)} %get-tuple-element.23.refs_0_, ...), custom_call_target="tpu_custom_call" | custom-call | tf_op jit(solution)/shard_map/pallas_call | solution.py:1196

commit v7 on v6

--- a/solution.py
+++ b/solution.py
@@ -841,14 +841,17 @@
     for b in ORDER[2:]:
         finish_branch(b, each_group)
 
-    n_pp = new(2)
+    n_pp = new(4)
     for image in range(2):
         for q in range(PIXELS // BLOCK):
             px = slice(q * BLOCK, (q + 1) * BLOCK)
             part = dot(r.wpt[:, 0:512], r.act[image, :, :, :, px].reshape(512, BLOCK))
             r.acc[image, :, :, px] = part[0:128].reshape(GROUPS, 16, BLOCK)
             r.pps[image, :, :, px] = part[128:256].astype(BF16).reshape(GROUPS, 16, BLOCK)
-        send(r.pps.at[image], r.pr.at[image], n_pp + image, sibling)
+            if q % 4 == 3:
+                span = halves[q // 4]
+                number = n_pp + 2 * image + q // 4
+                send(r.pps.at[image, :, :, span], r.pr.at[image, :, :, span], number, sibling)
 
     for image in range(2):
         for b in range(4):
@@ -856,7 +859,8 @@
 
     g_og.finish(lambda g: r.ogs.at[1 - x, g])
     for image in range(2):
-        arrived(r.pr.at[image], n_pp + image, sibling)
+        for n in range(2):
+            arrived(r.pr.at[image, :, :, halves[n]], n_pp + 2 * image + n, sibling)
 
     arrived(r.poolr, n_pool, sibling)
     for image in range(2):
@@ -1144,21 +1148,28 @@
     ]
     r.dgains_o[...] = r.dgains[...]
     r.dbiases_o[...] = r.dbiases[...]
+    for n, copy in taps:
+        copy.wait()
+        r.dwv[n : n + 3] = r.dwbv[n : n + 3].astype(F32)
+        store(r.dwv.at[pl.ds(n, 3)], r.dwa.at[pl.ds(n, 3)])
     for n in range(0, 27, 3):
         if n not in met:
             r.dwv[n : n + 3] = jnp.zeros((3, 128, 256), F32)
             store(r.dwv.at[pl.ds(n, 3)], r.dwa.at[pl.ds(n, 3)])
-    for n, copy in taps:
-        copy.wait()
-        r.dwv[n : n + 3] = r.dwbv[n : n + 3].astype(F32)
-        store(r.dwv.at[pl.ds(n, 3)], r.dwa.at[pl.ds(n, 3)])
     one.wait()
     r.dwv[27] = r.dwbv[27].astype(F32)
     store(r.dwv.at[27], r.dw1)
     fg.wait()
-    for h in range(ROWS):
-        r.fgv[pl.ds(h, 128, stride=16), :] = r.fgbv[:, h * 128 : (h + 1) * 128].astype(F32)
-    store(r.fgv, r.fg)
+    rr = iota((256, 256), 0)
+    cc = iota((256, 256), 1)
+    perm = jnp.where(cc == lax.rem(rr, 16) * 16 + lax.div(rr, 16), 1.0, 0.0).astype(BF16)
+    for block in range(8):
+        channels = slice(block * 16, (block + 1) * 16)
+        parts = [r.fgbv[channels, h * 128 : (h + 1) * 128] for h in range(ROWS)]
+        r.fgv[block * 256 : (block + 1) * 256] = dot(perm, jnp.concatenate(parts, axis=0))
+        if block % 4 == 3:
+            half = pl.ds((block - 3) * 256, 1024)
+            store(r.fgv.at[half], r.fg.at[half])
     for copy, name in passed:
         copy.wait()
         store(getattr(r, name + "v"), getattr(r, name + "_o"))

time: 108 us -> 107 us (level)
  no operation moved by 1% of the time
where the time goes in v7:
time: 107 us
  Pallas kernels  106 us (99%)
    pallas_call x1, Pallas kernels, fused(): pl.pallas_call(head_kernel, out_shape=shapes, in_specs=[hbm] * len(INPUTS...  101 us
    pallas_call x1, Pallas kernels, fused(): pl.pallas_call(copy_kernel, out_shape=[jax.ShapeDtypeStruct(s, F32) for s...  4.76 us

profile of v7, /device:TPU:0, one launch (start us, length us, event | category | flops | bytes accessed | tf_op | source)
XLA Modules:
  0.0 107.1 jit_solution(14980662494178657238)
XLA Ops:
  0.6 101.5 %shard_map.143 = (f32[256,128]{1,0:T(8,128)}, f32[128,256]{1,0:T(8,128)}, f32[5,16,256]{2,1,0:T(8,128)}, f32[5,16]{1,0:T(8,128)}, f32[5,16]{1,0:T(8,128)}, /*ind...) custom-call(bf16[2048,128]{1,0:T(8,128)(2,1)} %bitcast.7, bf16[256,128]{1,0:T(8,128)(2,1)} %bitcast.8, ...), custom_call_target="tpu_custom_call" | custom-call | tf_op jit(solution)/shard_map/pallas_call | solution.py:1187
  102.1 4.8 %shard_map.144 = (f32[256,128]{1,0:T(8,128)}, f32[128,256]{1,0:T(8,128)}, f32[5,16,256]{2,1,0:T(8,128)}, f32[5,16]{1,0:T(8,128)}, f32[5,16]{1,0:T(8,128)}, /*ind...) custom-call(f32[256,128]{1,0:T(8,128)} %get-tuple-element.23.refs_0_, ...), custom_call_target="tpu_custom_call" | custom-call | tf_op jit(solution)/shard_map/pallas_call | solution.py:1207
